TPU v7x, 32 devices: a whole 2x2x4 slice. The times are simulated.
32 devices in a mesh: dp: 8 (over y, x, core), vis: 4 (over z).
Axes of the slice: x: 2, y: 2, z: 4, core: 2. Of those that a mesh axis runs over, the one named last changes fastest.
Arguments:
- patches: bfloat16 [16384, 1280], P(('dp', 'vis')), may hold values from -100 to 100
- window_index: int32 [32, 512], P(('dp', 'vis')), may hold values from 0 to 511, each once within a row
- window_live: int32 [32, 8], P(('dp', 'vis')), may hold values from 0 to 64, as said below
- d_merged: bfloat16 [4096, 5120], P(('dp', 'vis')), may hold values from -1 to 1
- w_qkv: bfloat16 [1280, 2880], replicated, may hold values from -20 to 20
- w_out: bfloat16 [960, 1280], replicated, may hold values from -0.1875 to 0.1875
- merge_gain: float32 [1280], replicated, may hold values from 0.1 to 1.9
Outputs:
- merged: bfloat16 [4096, 5120], P(('dp', 'vis'))
- grad_qkv: float32 [1280, 2880], P(('dp', 'vis'))
- grad_out: float32 [960, 1280], P(None, ('dp', 'vis'))
- grad_gain: float32 [1280], P(('dp', 'vis'))
Inputs may be any that keep to these rules, and one draw needn't show every extreme that they name: `window_live`: entry [i, w] gives the live rows of window slot w of device i = dp * 4 + vis: 0 for an empty slot, else a multiple of 4. On every device the slots with live rows come first. In every vis column the 8 owners hold together exactly 32 windows with live rows.
All inputs are finite; a program needn't handle non-finite values.
Results may differ from a plain program's by a relative error of at most 0.018.
Values may be sent and summed in bfloat16 or wider, within the bound.
No kernel may reach another device: no remote copies, remote signals or barrier semaphores. Data moves between devices by JAX's collectives and lax.ppermute only.
A program may use at most 192 MiB of HBM per device.

v0:
```python
import jax
import jax.numpy as jnp
from jax import lax
from jax.sharding import PartitionSpec as P

HEADS = 12


EPSILON = 1e-06
NEGATIVE = -1e30


def contract(formula, first_op, second_op):
    return jnp.einsum(formula, first_op, second_op, preferred_element_type=jnp.float32)


def forward(window_rows, live_rows, w_qkv, w_out, merge_gain):
    window_count, win_rows, model_width = window_rows.shape
    inner_width = w_out.shape[0]
    head_width = inner_width // HEADS
    widened = window_rows.astype(jnp.float32)
    normed = (widened * lax.rsqrt(jnp.mean(widened * widened, -1, keepdims=True) + EPSILON)).astype(
        jnp.bfloat16
    )
    packed = contract("bwd,de->bwe", normed, w_qkv).astype(jnp.bfloat16)
    packed = packed.reshape(window_count, win_rows, 3, HEADS, head_width)
    query = packed[:, :, 0]
    key_rows = packed[:, :, 1]
    values = packed[:, :, 2]
    scores = contract("bqhc,bkhc->bhqk", query, key_rows) * head_width ** (-0.5)
    alive = jnp.arange(win_rows)[None, :] < live_rows[:, None]
    scores = jnp.where(alive[:, None, None, :], scores, NEGATIVE)
    probs = jax.nn.softmax(scores, axis=-1)
    probs_low = probs.astype(jnp.bfloat16)
    context = (
        contract("bhqk,bkhc->bqhc", probs_low, values)
        .astype(jnp.bfloat16)
        .reshape(window_count, win_rows, inner_width)
    )
    attended = widened + contract("bwi,id->bwd", context, w_out)
    inverse = lax.rsqrt(jnp.mean(attended * attended, -1, keepdims=True) + EPSILON)
    normalized = attended * inverse
    row_mask = alive[:, :, None].astype(jnp.float32)
    merged = (
        (normalized * merge_gain * row_mask)
        .astype(jnp.bfloat16)
        .reshape(window_count, win_rows // 4, 4 * model_width)
    )
    saved = (
        normed,
        query,
        key_rows,
        values,
        probs,
        probs_low,
        context,
        normalized,
        inverse,
        row_mask,
    )
    return (merged, saved)


def backward(saved, cotangent, w_out, merge_gain):
    normed, query, key_rows, values, probs, probs_low, context, normalized, inverse, row_mask = (
        saved
    )
    window_count, win_rows, model_width = normalized.shape
    head_width = query.shape[-1]
    grad_rows = (
        cotangent.astype(jnp.float32).reshape(window_count, win_rows, model_width) * row_mask
    )
    grad_gain = jnp.sum(grad_rows * normalized, axis=(0, 1))
    scaled = grad_rows * merge_gain
    d_attended = (
        inverse * (scaled - normalized * jnp.mean(scaled * normalized, -1, keepdims=True))
    ).astype(jnp.bfloat16)
    grad_out = contract("bwi,bwd->id", context, d_attended)
    d_context = (
        contract("bwd,id->bwi", d_attended, w_out)
        .astype(jnp.bfloat16)
        .reshape(window_count, win_rows, HEADS, head_width)
    )
    d_values = contract("bhqk,bqhc->bkhc", probs_low, d_context)
    d_probs = contract("bqhc,bkhc->bhqk", d_context, values)
    d_scores = (
        probs * (d_probs - jnp.sum(d_probs * probs, -1, keepdims=True)) * head_width ** (-0.5)
    ).astype(jnp.bfloat16)
    d_query = contract("bhqk,bkhc->bqhc", d_scores, key_rows)
    d_keys = contract("bhqk,bqhc->bkhc", d_scores, query)
    d_packed = (
        jnp.stack([d_query, d_keys, d_values], axis=2)
        .astype(jnp.bfloat16)
        .reshape(window_count, win_rows, -1)
    )
    grad_qkv = contract("bwd,bwe->de", normed, d_packed)
    return (grad_qkv, grad_out, grad_gain)


def on_device(patches, window_index, window_live, d_merged, w_qkv, w_out, merge_gain):
    model_width = patches.shape[1]
    slot_count = window_live.shape[1]
    win_rows = patches.shape[0] // slot_count
    window_rows = jnp.take(patches, window_index[0], axis=0).reshape(
        slot_count, win_rows, model_width
    )
    own_live = window_live[0]
    own_cot = d_merged.reshape(slot_count, win_rows // 4, 4 * model_width)
    ranks = lax.axis_size("dp")
    per_pair = max(1, slot_count // ranks)
    buffer_slots = ranks * per_pair
    capacity = slot_count // 2
    column_live = lax.all_gather(window_live, "dp", axis=0, tiled=True)
    counts = jnp.sum((column_live > 0).astype(jnp.int32), axis=1)
    starts = jnp.cumsum(counts) - counts
    my_rank = lax.axis_index("dp")
    slot_ids = jnp.arange(slot_count, dtype=jnp.int32)
    target = (starts[my_rank] + slot_ids) % ranks * per_pair + slot_ids // ranks
    buffer_ids = jnp.arange(buffer_slots, dtype=jnp.int32)
    route = ((target[None, :] == buffer_ids[:, None]) & (own_live > 0)[None, :]).astype(
        jnp.bfloat16
    )
    senders = buffer_ids // per_pair
    layers = buffer_ids % per_pair
    offsets = (my_rank - starts[senders]) % ranks + layers * ranks
    arrived = jnp.where(
        offsets < counts[senders], column_live[senders, jnp.minimum(offsets, slot_count - 1)], 0
    )
    flags = (arrived > 0).astype(jnp.int32)
    places = jnp.cumsum(flags) - flags
    chosen = (places[None, :] == jnp.arange(capacity, dtype=jnp.int32)[:, None]) & (flags > 0)[
        None, :
    ]
    picker = chosen.astype(jnp.bfloat16)
    vision_live = jnp.sum(jnp.where(chosen, arrived[None, :], 0), axis=1)
    out_rows = contract("sk,kf->sf", route, window_rows.reshape(slot_count, -1)).astype(
        jnp.bfloat16
    )
    out_cot = contract("sk,kf->sf", route, own_cot.reshape(slot_count, -1)).astype(jnp.bfloat16)
    in_rows = lax.all_to_all(out_rows, "dp", split_axis=0, concat_axis=0, tiled=True)
    vision_rows = (
        contract("cs,sf->cf", picker, in_rows)
        .astype(jnp.bfloat16)
        .reshape(capacity, win_rows, model_width)
    )
    vision_merged, saved = forward(vision_rows, vision_live, w_qkv, w_out, merge_gain)
    sent_back = contract("cs,cf->sf", picker, vision_merged.reshape(capacity, -1)).astype(
        jnp.bfloat16
    )
    returned = lax.all_to_all(sent_back, "dp", split_axis=0, concat_axis=0, tiled=True)
    merged = contract("sk,sf->kf", route, returned).astype(jnp.bfloat16)
    in_cot = lax.all_to_all(out_cot, "dp", split_axis=0, concat_axis=0, tiled=True)
    vision_cot = (
        contract("cs,sf->cf", picker, in_cot)
        .astype(jnp.bfloat16)
        .reshape(capacity, win_rows // 4, 4 * model_width)
    )
    grad_qkv, grad_out, grad_gain = backward(saved, vision_cot, w_out, merge_gain)
    total_qkv, total_out, total_gain = (
        lax.psum_scatter(grad_qkv, ("dp", "vis"), scatter_dimension=0, tiled=True),
        lax.psum_scatter(grad_out, ("dp", "vis"), scatter_dimension=1, tiled=True),
        lax.psum_scatter(grad_gain, ("dp", "vis"), scatter_dimension=0, tiled=True),
    )
    merged_rows = merged.reshape(slot_count * (win_rows // 4), 4 * model_width)
    return (merged_rows, total_qkv, total_out, total_gain)


def solution(mesh):
    in_specs = (
        P(("dp", "vis"), None),
        P(("dp", "vis"), None),
        P(("dp", "vis"), None),
        P(("dp", "vis"), None),
        P(),
        P(),
        P(),
    )
    out_specs = (
        P(("dp", "vis"), None),
        P(("dp", "vis"), None),
        P(None, ("dp", "vis")),
        P(("dp", "vis")),
    )
    return jax.shard_map(
        on_device, mesh=mesh, in_specs=in_specs, out_specs=out_specs, check_vma=False
    )
```

profile of v0, /device:TPU:0, one launch (start us, length us, event | category | flops | bytes accessed | tf_op | source)
XLA Modules:
  0.0 649.8 jit_solution(8013155950528379416)
XLA Ops:
  10.6 10.3 %all-gather = s32[8,1,8]{2,1,0:T(1,128)S(1)} all-gather(s32[1,1,8]{2,1,0:T(1,128)} %bitcast.145), channel_id=1, replica_groups=mesh['dp'=8,'vis'=4] {'dp'}, dimensions={0}, use_global_device_ids=true | all-gather | bytes 288 | tf_op jit(solution)/shard_map/all_gather | solution.py:113
  22.6 5.4 gather_fusion.3
  34.6 3.6 reduce.4
  41.7 4.3 all-to-all-start
  54.0 3.6 reduce.5
  64.2 4.3 all-to-all-start.2
  68.7 6.1 reshape.407
  80.7 6.0 all-to-all-done.2
  86.7 6.1 reshape.411
  92.8 4.5 fusion.6
  97.3 6.5 %fusion.9 = bf16[4,64,2880]{2,1,0:T(8,128)(2,1)} fusion(bf16[1280,2880]{0,1:T(8,128)(2,1)} %param.11, f32[1,4,64,1280]{3,1,2,0:T(4,128)S(1)} %bitcast.137, f32[4,64]{1,0:T(4,128)S(1)} %add_rsqrt_fusion.1), kind=kOutput, calls=%fused_computation.21 | convolution fusion | flops 1888829440 | bytes 10159104 | tf_op jit(solution)/shard_map/bwd,de->bwe/dot_general | solution.py:14
  103.8 6.3 reshape.355
  110.2 3.8 fusion.92
  113.9 4.6 fusion.93
  134.7 4.6 fusion.49
  139.2 4.6 fusion.46
  154.1 5.1 convert_element_type.137
  162.3 7.6 %convolution_bitcast_fusion = f32[1280,2880]{1,0:T(8,128)} fusion(bf16[4,64,2880]{2,1,0:T(8,128)(2,1)S(1)} %copy-done.12, bf16[1,4,64,1280]{3,1,2,0:T(4,128)(2,1)S(1)} %bitcast.143), kind=kOutput, calls=%fused_computation.17 | convolution fusion | flops 1887436800 | bytes 16875520 | tf_op jit(solution)/shard_map/bwd,bwe->de/dot_general | solution.py:14
  177.9 3.6 all-to-all-start.1
  181.4 55.8 %all-reduce.1 = f32[1280]{0:T(1024)S(1)} all-reduce(f32[1280]{0:T(1024)S(1)} %get-tuple-element.4), channel_id=4, replica_groups=mesh['dp'=8,'vis'=4] {'dp','vis'}, use_global_device_ids=true, to_apply=%region_13.14.clone | all-reduce | flops 1280 | bytes 10240
  237.8 3.7 reshape.409
  241.5 4.5 convolution_convert_fusion.1
  249.0 64.0 %reduce-scatter.6.cloned.1.call-done = f32[960,40]{0,1:T(8,128)} async-done(((f32[960,1280]{0,1:T(8,128)}), f32[960,40]{0,1:T(8,128)}) %reduce-scatter.6.cloned.1.call-update) | async-done | bytes 153616 | tf_op jit(solution)/shard_map/reduce_scatter | solution.py:161
  313.0 329.6 %reduce-scatter.8.cloned.1.call-done = f32[40,2880]{1,0:T(8,128)} async-done(((f32[1280,2880]{1,0:T(8,128)}), f32[40,2880]{1,0:T(8,128)}) %reduce-scatter.8.cloned.1.call-update) | async-done | bytes 460816
  (104 shorter events, 76.9 us)
Async XLA Ops:
  7.2 117.1 %copy-start = (bf16[960,1280]{1,0:T(8,128)(2,1)S(1)}, bf16[960,1280]{1,0:T(8,128)(2,1)}, u32[]{:S(2)}) copy-start(bf16[960,1280]{1,0:T(8,128)(2,1)} %param.12) | copy-start | bytes 7372804
  41.7 22.5 %all-to-all-start = ((bf16[8,2,40960]{2,1,0:T(2,128)(2,1)}), bf16[8,2,40960]{2,1,0:T(2,128)(2,1)}, u32[]{:S(2)}, u32[]{:S(2)}) async-start(bf16[8,2,40960]{2,1,0:T(2,128)(2,1)} %reshape.406), calls=%async_computation | async-start | bytes 2621440 | tf_op jit(solution)/shard_map/all_to_all | solution.py:140
  64.2 22.5 %all-to-all-start.2 = ((bf16[8,2,40960]{2,1,0:T(2,128)(2,1)}), bf16[8,2,40960]{2,1,0:T(2,128)(2,1)}, u32[]{:S(2)}, u32[]{:S(2)}) async-start(bf16[8,2,40960]{2,1,0:T(2,128)(2,1)} %reshape.410), calls=%async_computation.2 | async-start | bytes 2621440 | tf_op jit(solution)/shard_map/all_to_all | solution.py:152
  68.5 244.5 %reduce-scatter.6.cloned.1.call-start = ((), (), s32[]{:S(2)}) async-start(), calls=%async_computation.5 | async-start | bytes 5406720 | tf_op jit(solution)/shard_map/reduce_scatter | solution.py:161
  78.1 1.1 copy-start.2
  92.8 4.6 copy-start.3
  113.9 4.6 copy-start.7
  124.3 2.5 copy-start.5
  124.3 2.5 copy-start.16
  128.6 0.9 copy-start.9
  130.4 1.2 copy-start.8
  131.7 1.7 copy-start.17
  131.7 1.7 copy-start.18
  133.4 1.3 copy-start.14
  134.7 4.6 copy-start.13
  139.2 4.6 copy-start.10
  143.8 3.2 copy-start.6
  147.0 1.9 copy-start.15
  159.2 1.3 copy-start.4
  159.2 483.3 %reduce-scatter.8.cloned.1.call-start = ((), (), s32[]{:S(2)}) async-start(), calls=%async_computation.6 | async-start | bytes 15544320
  160.5 1.8 copy-start.12
  169.9 1.1 copy-start.11
  177.9 60.0 %all-to-all-start.1 = ((bf16[8,2,40960]{2,1,0:T(2,128)(2,1)}), bf16[8,2,40960]{2,1,0:T(2,128)(2,1)S(1)}, u32[]{:S(2)}, u32[]{:S(2)}) async-start(bf16[8,2,40960]{2,1,0:T(2,128)(2,1)} %reshape.408), calls=%async_computation.1 | async-start | bytes 2621440 | tf_op jit(solution)/shard_map/all_to_all | solution.py:150
  241.5 401.0 %copy-start.1 = (bf16[960,1280]{1,0:T(8,128)(2,1)S(1)}, bf16[960,1280]{1,0:T(8,128)(2,1)}, u32[]{:S(2)}) copy-start(bf16[960,1280]{1,0:T(8,128)(2,1)} %param.12) | copy-start | bytes 7372804
Sparse Core Ops, SparseCore 0:
  159.3 153.6 reduce-scatter.5
  315.9 326.6 reduce-scatter.7
where the time goes:
time: 658 us; the launch traced here: 650 us
  waiting for transfers between devices  402 us (61%)
  local copies, waits for them, and re-layouts  76.5 us (12%)
  blocking collectives  66.1 us (10%)
  matrix products  57.8 us (9%)
  other arithmetic  19.7 us (3%)
  between operations  14.7 us (2%)
  starting transfers between devices  12.6 us (2%)
    unnamed x3, waiting for transfers between devices  330 us
    reduce_scatter x1, waiting for transfers between devices, on_device(): lax.psum_scatter(grad_out, ('dp', 'vis'), scatter_dimension=1, tiled=True)  64 us
    unnamed x1, blocking collectives  55.8 us
    dot_general x16, matrix products, contract(): jnp.einsum(formula, first_op, second_op, preferred_element_type=jnp.float32)  53.3 us
    unnamed x49, local copies, waits for them, and re-layouts  35.2 us
  transfers between devices with their start and end apart: 5, of which 4 were waited for; matrix products, arithmetic and copies ran while one was open for 8% of the time, Pallas kernels for 0%

commit v1 on v0

v1 whole, which is shorter than its diff:
```python
import functools

import jax
import jax.numpy as jnp
from jax import lax
from jax.experimental import pallas as pl
from jax.experimental.pallas import tpu as pltpu
from jax.sharding import PartitionSpec as P

HEADS = 12
STAGE = 4
PARTS = 3
JOIN = 4
PAIR = 2
LANES = 128
TILE = 256
EPSILON = 1e-06
NEGATIVE = -1e30
F32 = jnp.float32
BF16 = jnp.bfloat16


def ceil_to(size, step):
    return -(-size // step) * step


def dot(left, right, left_axis=1, right_axis=0):
    return lax.dot_general(
        left, right, (((left_axis,), (right_axis,)), ((), ())), preferred_element_type=F32
    )


def tiles(width, step=TILE):
    return [(at, min(step, width - at)) for at in range(0, width, step)]


def alive_of(place, live_first, live_second, group):
    limit = jnp.where((place // group) % PAIR == 0, live_first, live_second)
    return (place % group) * JOIN < limit


def forward_kernel(
    rank_ref, live_ref, index_ref, patches_ref, gain_ref, cot_hbm, w_qkv_hbm, w_out_hbm,
    merged_hbm, packed_hbm, probs_hbm, d_context_hbm, context_hbm,
    norm_keep_hbm, norm_send_hbm, att_keep_hbm, att_send_hbm,
    cot_ref, w_qkv_ref, w_out_ref,
    merged_ref, packed_ref, probs_ref, d_context_ref, context_ref,
    norm_keep_ref, norm_send_ref, att_keep_ref, att_send_ref,
    rows_ref, norm_ref, turned_ref, upright_ref, d_att_ref, gain_sum_ref, place_ref, chosen_ref,
    in_sems, out_sems,
):
    row_count, model_width = patches_ref.shape
    inner = w_out_ref.shape[0]
    head_width = inner // HEADS
    slots = live_ref.shape[1]
    win_rows = row_count // slots
    group = win_rows // JOIN
    block = PAIR * win_rows
    strip = PAIR * group
    pairs = slots // PAIR
    scale = head_width ** (-0.5)
    outs = {}

    parts = tiles(3 * inner, inner // 2)
    loads = [
        pltpu.make_async_copy(
            w_qkv_hbm.at[pl.ds(at, size)], w_qkv_ref.at[pl.ds(at, size)], in_sems.at[n]
        )
        for n, (at, size) in enumerate(parts)
    ]
    load_out = pltpu.make_async_copy(w_out_hbm, w_out_ref, in_sems.at[len(parts)])
    load_cot = pltpu.make_async_copy(cot_hbm, cot_ref, in_sems.at[len(parts) + 1])
    for load in loads + [load_out, load_cot]:
        load.start()

    def give(n, source, target):
        outs[n] = pltpu.make_async_copy(source, target, out_sems.at[n])
        outs[n].start()

    def by_core(source, keep, send):
        half, rank_rows, _ = keep.shape
        core, chip = rank_ref[0] & 1, rank_ref[0] >> 1
        for rank in range(2 * half):
            piece = source[rank * rank_rows:(rank + 1) * rank_rows, :]

            @pl.when(core == rank % 2)
            def _():
                keep[chip ^ (rank // 2)] = piece

            @pl.when(core != rank % 2)
            def _():
                send[chip ^ (rank // 2)] = piece

    places = jnp.broadcast_to(index_ref[...].astype(F32), (LANES, row_count))
    place_ref[...] = places.T
    raster = lax.broadcasted_iota(jnp.int32, (strip, row_count), 1)
    for pair in range(pairs):
        for turn in range(JOIN):
            at = pair * block + turn * strip
            place = place_ref[pl.ds(pair * block + turn, strip, stride=JOIN), :]
            found = raster == place[:, :1].astype(jnp.int32)
            chosen_ref[at:at + strip, :] = jnp.where(found, 1.0, 0.0).astype(BF16)
    for at, size in tiles(model_width):
        rows_ref[:, at:at + size] = dot(chosen_ref[...], patches_ref[:, at:at + size])

    for pair in range(pairs):
        here = slice(pair * block, (pair + 1) * block)
        rows = rows_ref[here, :]
        power = jnp.mean(rows * rows, axis=1, keepdims=True)
        normed = (rows * lax.rsqrt(power + EPSILON)).astype(BF16)
        norm_ref[:, here] = normed.T
    by_core(norm_ref, norm_keep_ref, norm_send_ref)
    give(0, norm_keep_ref, norm_keep_hbm)
    give(1, norm_send_ref, norm_send_hbm)

    for load, (first, height) in zip(loads, parts):
        load.wait()
        for at, size in tiles(height):
            at += first
            found = dot(w_qkv_ref[at:at + size, :], norm_ref[...]).astype(BF16)
            part, at = at // inner, at % inner
            for pair in range(pairs):
                packed_ref[pair, part, at:at + size, :] = found[:, pair * block:(pair + 1) * block]
    give(2, packed_ref, packed_hbm)

    @pl.loop(0, pairs)
    def _(pair):
        here = pl.ds(pl.multiple_of(pair * block, block), block)
        key_at = lax.broadcasted_iota(jnp.int32, (block, block), 0)
        query_at = lax.broadcasted_iota(jnp.int32, (block, block), 1)
        allowed = alive_of(key_at, live_ref[0, PAIR * pair], live_ref[0, PAIR * pair + 1], group)
        allowed = allowed & ((key_at // group) % PAIR == (query_at // group) % PAIR)
        for first in range(0, HEADS, STAGE):
            spans = [
                slice(head * head_width, (head + 1) * head_width)
                for head in range(first, first + STAGE)
            ]
            scores = [
                dot(packed_ref[pair, 1, span, :], packed_ref[pair, 0, span, :], 0, 0)
                for span in spans
            ]
            probs = []
            for one in scores:
                one = jnp.where(allowed, one, NEGATIVE)
                grown = jnp.exp((one - jnp.max(one, axis=0, keepdims=True)) * scale)
                one = grown * (1.0 / jnp.sum(grown, axis=0, keepdims=True))
                probs.append(one.astype(BF16))
            found = [dot(packed_ref[pair, 2, span, :], one) for span, one in zip(spans, probs)]
            for n, span in enumerate(spans):
                probs_ref[pair, first + n] = probs[n]
                context_ref[span, here] = found[n].astype(BF16)

    give(3, probs_ref, probs_hbm)
    give(4, context_ref, context_hbm)
    for pair in range(pairs):
        here = slice(pair * block, (pair + 1) * block)
        upright_ref[here, :] = context_ref[:, here].T
    load_out.wait()
    for at, size in tiles(model_width):
        rows_ref[:, at:at + size] += dot(upright_ref[...], w_out_ref[:, at:at + size])

    gain_sum_ref[...] = jnp.zeros_like(gain_sum_ref)
    load_cot.wait()

    @pl.loop(0, pairs)
    def _(pair):
        row_at = lax.broadcasted_iota(jnp.int32, (strip, 1), 0)
        alive = alive_of(row_at, live_ref[0, PAIR * pair], live_ref[0, PAIR * pair + 1], group)
        alive = jnp.where(alive, 1.0, 0.0)
        gain = gain_ref[...]
        out_rows = pl.ds(pl.multiple_of(pair * strip, strip), strip)
        for turn in range(JOIN):
            here = pl.ds(pl.multiple_of(pair * block + turn * strip, strip), strip)
            columns = slice(turn * model_width, (turn + 1) * model_width)
            attended = rows_ref[here, :]
            power = jnp.mean(attended * attended, axis=1, keepdims=True)
            inverse = lax.rsqrt(power + EPSILON)
            normalized = attended * inverse
            merged_ref[out_rows, columns] = (normalized * gain * alive).astype(BF16)
            grad_rows = cot_ref[out_rows, columns].astype(F32) * alive
            crossed = grad_rows * normalized
            gain_sum_ref[...] += jnp.sum(crossed.reshape(strip // 8, 8, model_width), axis=0)
            mean = jnp.mean(crossed * gain, axis=1, keepdims=True)
            d_att_ref[here, :] = (inverse * (grad_rows * gain - normalized * mean)).astype(BF16)

    give(5, merged_ref, merged_hbm)
    total = jnp.sum(gain_sum_ref[...], axis=0, keepdims=True)
    high = total.astype(BF16).astype(F32)
    at_row = lax.broadcasted_iota(jnp.int32, (LANES, model_width), 0)
    tail = jnp.where(at_row == 0, high, jnp.where(at_row == 1, total - high, 0.0))
    d_att_ref[row_count:, :] = tail.astype(BF16)

    for at, size in tiles(row_count + LANES, LANES):
        turned_ref[:, at:at + size] = d_att_ref[at:at + size, :].T
    by_core(turned_ref, att_keep_ref, att_send_ref)
    give(6, att_keep_ref, att_keep_hbm)
    give(7, att_send_ref, att_send_hbm)

    for at, size in tiles(inner):
        found = dot(w_out_ref[at:at + size, :], turned_ref[:, :row_count]).astype(BF16)
        for pair in range(pairs):
            d_context_ref[pair, at:at + size, :] = found[:, pair * block:(pair + 1) * block]
    give(8, d_context_ref, d_context_hbm)
    for n in sorted(outs):
        outs[n].wait()


def backward_kernel(*refs):
    for packed_ref, probs_ref, d_context_ref, d_packed_ref in zip(*[iter(refs)] * 4):
        _, heads, block, _ = probs_ref.shape
        height = d_context_ref.shape[1]
        head_width = height // heads
        scale = head_width ** (-0.5)
        spans = [slice(head * head_width, (head + 1) * head_width) for head in range(heads)]
        probs = [probs_ref[0, head] for head in range(heads)]
        d_probs = [
            dot(packed_ref[0, 2, 0, span, :], d_context_ref[0, span, :], 0, 0) for span in spans
        ]
        d_scores = []
        for low, one in zip(probs, d_probs):
            exact = low.astype(F32)
            inside = jnp.sum(one * exact, axis=0, keepdims=True)
            d_scores.append((exact * (one - inside) * scale).astype(BF16))
        founds = (
            [dot(packed_ref[0, 1, 0, span, :], one) for span, one in zip(spans, d_scores)],
            [dot(packed_ref[0, 0, 0, span, :], one, 1, 1) for span, one in zip(spans, d_scores)],
            [dot(d_context_ref[0, span, :], one, 1, 1) for span, one in zip(spans, probs)],
        )
        for n, found in enumerate(founds):
            for span, one in zip(spans, found):
                d_packed_ref[n * height + span.start:n * height + span.stop, :] = one.astype(BF16)


def product_kernel(*refs, taken, spans, extra_at):
    keep_ref, other_ref = refs[:2]
    rights = refs[2:-2]
    outs = refs[-2:]
    rank_rows, width = outs[0].shape[1:]
    depth = rights[0].shape[1]
    whole = rank_rows % 16 == 0
    lists = [[(n, g) for g in places] for n, places in enumerate(taken)]
    lists = [lists[0] + lists[1]] if whole else [[one] for one in lists[0] + lists[1]]
    count = len(rights) // 2
    sides = []
    for side in range(2):
        pieces = [
            ref[first:last] for ref, (first, last) in zip(rights[side * count:], spans)
        ]
        sides.append(jnp.concatenate(pieces, axis=0) if count > 1 else pieces[0])
    for ordered in lists:
        lefts = []
        for ref in (keep_ref, other_ref):
            pieces = [ref[g] for _, g in ordered]
            lefts.append(jnp.concatenate(pieces, axis=0) if whole else pieces[0])
        for at, size in tiles(sides[0].shape[0], 2 * TILE):
            total = dot(lefts[0][:, :depth], sides[0][at:at + size], 1, 1)
            total += dot(lefts[1][:, :depth], sides[1][at:at + size], 1, 1)
            place = [0, 0]
            for n, (side, g) in enumerate(ordered):
                spot = taken[side].index(g)
                outs[side][spot, :, at:at + size] = total[
                    n * rank_rows:(n + 1) * rank_rows
                ].astype(BF16)
        if extra_at is not None:
            column = lax.broadcasted_iota(jnp.int32, (LANES, LANES), 1)
            ones = jnp.where(column == extra_at % LANES, 1.0, 0.0).astype(BF16)
            total = dot(lefts[0][:, depth:], ones) + dot(lefts[1][:, depth:], ones)
            for n, (side, g) in enumerate(ordered):
                spot = taken[side].index(g)
                outs[side][spot, :, extra_at:] = total[
                    n * rank_rows:(n + 1) * rank_rows, extra_at % LANES:
                ].astype(BF16)


def product(left, own, theirs, spans, bit, extra_at=None):
    keep, other = left
    half, rank_rows, _ = keep.shape
    depth = own[0].shape[1]
    columns = sum(last - first for first, last in spans)
    width = columns if extra_at is None else ceil_to(columns + 1, LANES)
    sent = [g for g in range(half) if (g >> (bit - 1)) & 1]
    kept = [g for g in range(half) if g not in sent]
    shape = jax.ShapeDtypeStruct((half // 2, rank_rows, width), BF16)
    return pl.pallas_call(
        functools.partial(product_kernel, taken=(sent, kept), spans=spans, extra_at=extra_at),
        out_shape=[shape, shape],
        in_specs=[VMEM] * (2 + 2 * len(own)),
        out_specs=[VMEM] * 2,
        compiler_params=pltpu.CompilerParams(vmem_limit_bytes=20 * 2**20),
        cost_estimate=SMALL,
    )(keep, other, *own, *theirs)


def flip_pairs(size, bit):
    return [(i, i ^ (1 << bit)) for i in range(size)]


def pick(array, place, axis):
    return lax.dynamic_index_in_dim(array, place, axis, keepdims=False)


def add_low(first, second):
    return (first.astype(F32) + second.astype(F32)).astype(BF16)


class Sum:
    def __init__(self, kept, got, order):
        self.ranks, self.layers = lax.axis_size("dp"), lax.axis_size("vis")
        self.order = order[1:]
        self.left = [b for b in range(len(order), 0, -1) if b != order[0]]
        shape = (2,) * len(self.left) + kept.shape[1:]
        self.kept, self.got = kept.reshape(shape), [got.reshape(shape)]

    def after(self, other):
        *self.got, other = lax.optimization_barrier((*self.got, other))
        return other

    def step(self):
        got = self.got[0]
        if self.order:
            bit, *self.order = self.order
            axis = self.left.index(bit)
            halves = [
                [lax.index_in_dim(array, n, axis, keepdims=False) for n in range(2)]
                for array in (self.kept, got)
            ]
            sent = add_low(halves[0][1], halves[1][1])
            self.got = [lax.ppermute(sent, "dp", flip_pairs(self.ranks, bit))]
            self.kept = add_low(halves[0][0], halves[1][0])
            self.left.remove(bit)
            return
        self.kept, self.got = add_low(self.kept, got), []


class Spread:
    def __init__(self, wholes):
        layers, layer = lax.axis_size("vis"), lax.axis_index("vis")
        shards = [whole.reshape(layers, -1, whole.shape[-1]) for whole in wholes]

        def row_of(k):
            place = (layer + k) % layers
            return jnp.concatenate([pick(one, place, 0) for one in shards], axis=-1)

        self.kept = row_of(0)
        self.got = []
        for k in range(1, layers):
            pairs = [(i, (i + k) % layers) for i in range(layers)]
            self.got.append(lax.ppermute(row_of(k), "vis", pairs))

    def total(self):
        total = self.kept.astype(F32)
        for one in self.got:
            total = total + one.astype(F32)
        return total


VMEM = pl.BlockSpec(memory_space=pltpu.VMEM)
SMEM = pl.BlockSpec(memory_space=pltpu.SMEM)
ANY = pl.BlockSpec(memory_space=pl.ANY)


SMALL = pl.CostEstimate(flops=1, bytes_accessed=1, transcendentals=0)


def run_forward(rank, window_live, window_index, patches, gain, d_merged, w_qkv, w_out, half):
    row_count, model_width = patches.shape
    inner = w_out.shape[0]
    slots = window_live.shape[1]
    block = PAIR * row_count // slots
    pairs = slots // PAIR
    rank_rows = model_width // (2 * half)
    shapes = [
        d_merged.shape,
        (pairs, 3, inner, block),
        (pairs, HEADS, block, block),
        (pairs, inner, block),
        (inner, row_count),
        (half, rank_rows, row_count),
        (half, rank_rows, row_count),
        (half, rank_rows, row_count + LANES),
        (half, rank_rows, row_count + LANES),
    ]
    loads = 2 + len(tiles(3 * inner, inner // 2))
    return pl.pallas_call(
        forward_kernel,
        out_shape=[jax.ShapeDtypeStruct(s, BF16) for s in shapes],
        in_specs=[SMEM, SMEM, VMEM, VMEM, VMEM, ANY, ANY, ANY],
        out_specs=[ANY] * len(shapes),
        scratch_shapes=[pltpu.VMEM(a.shape, BF16) for a in (d_merged, w_qkv, w_out)]
        + [pltpu.VMEM(s, BF16) for s in shapes]
        + [
            pltpu.VMEM((row_count, model_width), F32),
            pltpu.VMEM((model_width, row_count), BF16),
            pltpu.VMEM((model_width, row_count + LANES), BF16),
            pltpu.VMEM((row_count, inner), BF16),
            pltpu.VMEM((row_count + LANES, model_width), BF16),
            pltpu.VMEM((8, model_width), F32),
            pltpu.VMEM((row_count, LANES), F32),
            pltpu.VMEM((row_count, row_count), BF16),
            pltpu.SemaphoreType.DMA((loads,)),
            pltpu.SemaphoreType.DMA((len(shapes),)),
        ],
        compiler_params=pltpu.CompilerParams(vmem_limit_bytes=58 * 2**20),
        cost_estimate=SMALL,
    )(rank, window_live, window_index, patches, gain, d_merged, w_qkv, w_out)


def run_backward(packed, probs, d_context, taken):
    pairs, _, inner, block = packed.shape
    heads, height = HEADS // PARTS, inner // PARTS

    def specs(part):
        return [
            pl.BlockSpec((1, 3, 1, height, block), lambda n: (n, 0, part, 0, 0)),
            pl.BlockSpec((1, heads, block, block), lambda n: (n, part, 0, 0)),
            pl.BlockSpec((1, height, block), lambda n: (n, part, 0)),
        ]

    def body(*refs):
        ins, outs = refs[:3 * len(taken)], refs[3 * len(taken):]
        backward_kernel(*[
            ref for n in range(len(taken)) for ref in (*ins[3 * n:3 * n + 3], outs[n])
        ])

    packed = packed.reshape(pairs, 3, PARTS, height, block)
    return pl.pallas_call(
        body,
        out_shape=[jax.ShapeDtypeStruct((3 * height, pairs * block), BF16) for _ in taken],
        grid=(pairs,),
        in_specs=[spec for part in taken for spec in specs(part)],
        out_specs=[pl.BlockSpec((3 * height, block), lambda n: (0, n)) for _ in taken],
        compiler_params=pltpu.CompilerParams(vmem_limit_bytes=56 * 2**20),
        cost_estimate=SMALL,
    )(*[packed, probs, d_context] * len(taken))


def on_device(patches, window_index, window_live, d_merged, w_qkv, w_out, merge_gain):
    model_width = patches.shape[1]
    inner = w_out.shape[0]
    ranks = lax.axis_size("dp")
    rank = lax.axis_index("dp")
    bits = ranks.bit_length() - 2
    after = lax.optimization_barrier
    (
        merged, packed, probs, d_context, context, norm_keep, norm_send, att_keep, att_send
    ) = run_forward(
        rank.reshape(1), window_live, window_index, patches,
        merge_gain.reshape(1, model_width), d_merged, w_qkv.T, w_out, ranks // 2,
    )

    def swap(array, bit=0):
        return lax.ppermute(array, "dp", flip_pairs(ranks, bit))

    along = list(range(1, bits + 1))
    by_x = along
    by_y = along[bits // 2:] + along[:bits // 2]
    height = inner // PARTS
    rest = 3 * height % LANES
    full = 3 * height - rest

    att_got, context_got, norm_got = swap(att_send), swap(context), swap(norm_send)
    (d_first,) = run_backward(packed, probs, d_context, (0,))
    first_got = swap(d_first)

    context_got, d_first = after((context_got, d_first))
    sent, kept_out = product(
        (att_keep, att_got), [context], [context_got], [(0, inner)], by_x[0], inner
    )
    sum_out = Sum(kept_out, swap(sent, by_x[0]), by_x)

    first_got, kept_out = after((first_got, kept_out))
    norm = (norm_keep, norm_got)
    sent, kept_1 = product(norm, [d_first], [first_got], [(0, full)], by_y[0])
    sum_1 = Sum(kept_1, swap(sent, by_y[0]), by_y)

    probs, kept_1 = after((probs, kept_1))
    d_second, d_third = run_backward(packed, probs, d_context, (1, 2))
    d_second = sum_out.after(d_second)
    second_got = swap(d_second)
    d_third = sum_1.after(d_third)
    third_got = swap(d_third)

    sum_out.step()
    sent, kept_2 = product(
        norm, [d_second, d_first], [second_got, first_got],
        [(0, 3 * height), (full, 3 * height)], by_x[0],
    )
    sum_2 = Sum(kept_2, swap(sent, by_x[0]), by_x)

    sum_1.step()
    third_got, kept_2 = after((third_got, kept_2))
    sent, kept_3 = product(norm, [d_third], [third_got], [(0, 3 * height)], by_y[0])
    kept_3 = sum_1.after(kept_3)
    kept_3 = sum_out.after(kept_3)
    sum_3 = Sum(kept_3, swap(sent, by_y[0]), by_y)

    for _ in range(bits - 2):
        for one in (sum_out, sum_1, sum_2, sum_3):
            one.step()
    sum_out.step()
    sum_1.step()
    early = Spread([sum_out.kept, sum_1.kept])
    early.kept = sum_2.after(early.kept)
    sum_2.step()
    early.kept = sum_3.after(early.kept)
    sum_3.step()
    total = early.total()
    total = sum_2.after(total)
    total = sum_3.after(total)
    sum_2.step()
    sum_3.step()
    width = sum_out.kept.shape[-1]
    total_out, total_1 = total[:, :width], total[:, width:]
    total = Spread([sum_2.kept, sum_3.kept]).total()
    width = sum_2.kept.shape[-1]
    total_2, total_3 = total[:, :width], total[:, width:]

    columns = []
    for part in range(3):
        at = part * height
        columns.append(total_1[:, at:min(at + height, full)])
        if part == 2 and rest:
            columns.append(total_2[:, 3 * height:])
        columns += [total_2[:, at:at + height], total_3[:, at:at + height]]
    total_qkv = jnp.concatenate(columns, axis=-1)
    return (merged, total_qkv, total_out[:, :inner].T, total_out[:, inner])


def solution(mesh):
    in_specs = (
        P(("dp", "vis"), None),
        P(("dp", "vis"), None),
        P(("dp", "vis"), None),
        P(("dp", "vis"), None),
        P(),
        P(),
        P(),
    )
    out_specs = (
        P(("dp", "vis"), None),
        P(("dp", "vis"), None),
        P(None, ("dp", "vis")),
        P(("dp", "vis")),
    )
    return jax.shard_map(
        on_device, mesh=mesh, in_specs=in_specs, out_specs=out_specs, check_vma=False
    )
```

time: 658 us -> 108 us (0.16); the launches traced: 650 us -> 108 us
  waiting for transfers between devices: 402 us -> 33.7 us
  local copies, waits for them, and re-layouts: 76.5 us -> 5.25 us
  blocking collectives: 66.1 us -> 0 us
  matrix products: 57.8 us -> 0 us
  Pallas kernels: 0 us -> 40.5 us
  other arithmetic: 19.7 us -> 4.58 us
  between operations: 14.7 us -> 0.92 us
  starting transfers between devices: 12.6 us -> 22.6 us
    unnamed x3 -> x0, waiting for transfers between devices: 330 us -> none
    reduce_scatter x1 -> x0, waiting for transfers between devices: 64 us -> none  [on_device(): lax.psum_scatter(grad_out, ('dp', 'vis'), scatter_dimension=1, tiled=True)]
    unnamed x1 -> x0, blocking collectives: 55.8 us -> none
    dot_general x16 -> x0, matrix products: 53.3 us -> none  [contract(): jnp.einsum(formula, first_op, second_op, preferred_element_type=jnp.float32)]
    pallas_call x0 -> x7, Pallas kernels: none -> 40.5 us  [the longest x1 19.4 us: run_forward(): pl.pallas_call(forward_kernel, out_shape=[jax.ShapeDtypeStruct(s, BF16) f...]
    unnamed x49 -> x32, local copies, waits for them, and re-layouts: 35.2 us -> 1.26 us
    ppermute x0 -> x20, waiting for transfers between devices: none -> 33.7 us  [the longest x10 21.3 us: swap(): return lax.ppermute(array, 'dp', flip_pairs(ranks, bit))]
    ppermute x0 -> x20, starting transfers between devices: none -> 22.6 us  [the longest x6 11.4 us: __init__(): self.got.append(lax.ppermute(row_of(k), 'vis', pairs))]
  transfers between devices with their start and end apart: 5 -> 20, of which waited for: 4 -> 9; matrix products, arithmetic and copies ran while one was open for 8% -> 3% of each run, Pallas kernels for 0% -> 20%
where the time goes in v1:
time: 108 us
  Pallas kernels  40.5 us (38%)
  waiting for transfers between devices  33.7 us (31%)
  starting transfers between devices  22.6 us (21%)
  local copies, waits for them, and re-layouts  5.25 us (5%)
  other arithmetic  4.58 us (4%)
    ppermute x10, waiting for transfers between devices, swap(): return lax.ppermute(array, 'dp', flip_pairs(ranks, bit))  21.3 us
    pallas_call x1, Pallas kernels, run_forward(): pl.pallas_call(forward_kernel, out_shape=[jax.ShapeDtypeStruct(s, BF16) f...  19.4 us
    ppermute x6, starting transfers between devices, __init__(): self.got.append(lax.ppermute(row_of(k), 'vis', pairs))  11.4 us
    pallas_call x2, Pallas kernels, run_backward(): pl.pallas_call(body, out_shape=[jax.ShapeDtypeStruct((3 * height, pairs *...  11.3 us
    pallas_call x4, Pallas kernels, product(): pl.pallas_call(functools.partial(product_kernel, taken=(sent, kept), span...  9.78 us
    ppermute x10, starting transfers between devices, swap(): return lax.ppermute(array, 'dp', flip_pairs(ranks, bit))  7.17 us
    ppermute x4, waiting for transfers between devices, step(): self.got = [lax.ppermute(sent, 'dp', flip_pairs(self.ranks, bit))]  6.68 us
    ppermute x6, waiting for transfers between devices, __init__(): self.got.append(lax.ppermute(row_of(k), 'vis', pairs))  5.73 us
  transfers between devices with their start and end apart: 20, of which 9 were waited for; matrix products, arithmetic and copies ran while one was open for 3% of the time, Pallas kernels for 20%

profile of v1, /device:TPU:0, one launch (start us, length us, event | category | flops | bytes accessed | tf_op | source)
XLA Modules:
  0.0 107.5 jit_solution(7627581787140707414)
XLA Ops:
  0.6 1.3 %reshape.71.gain_ref = f32[1,1280]{1,0:T(1,128)} reshape(f32[1280]{0:T(1024)} %param.13) | data formatting | bytes 10240 | tf_op jit(solution)/shard_map/reshape | solution.py:448
  1.9 19.4 %shard_map.102 = (bf16[128,5120]{1,0:T(8,128)(2,1)}, bf16[4,3,960,128]{3,2,1,0:T(8,128)(2,1)}, bf16[4,12,128,128]{3,2,1,0:T(8,128)(2,1)}, bf16[4,960,128]{2,1,0:...) custom-call(s32[1]{0:T(128)} %bitcast.rank_ref, ...), custom_call_target="tpu_custom_call" | custom-call | flops 1 | bytes 1 | tf_op jit(solution)/shard_map/pallas_call | solution.py:384
  21.8 5.0 %shard_map.103.refs_2_.refs_3_ = bf16[960,512]{1,0:T(8,128)(2,1)} custom-call(bf16[4,3,3,320,128]{4,3,2,1,0:T(8,128)(2,1)} %bitcast.69, bf16[4,12,128,128]{3,2,1,0:T(8,128)(2,1)} %get-tuple-element.59.refs_1_.refs_4_, bf16[4,960,128]{2,1,0:T(8,128)(2,1)} %get-tuple-element.50.refs_2_.refs_5_), custom_call_target="tpu_custom_call" | custom-call | flops 1 | bytes 1 | tf_op jit(solution)/shard_map/pallas_call | solution.py:426
  27.4 3.8 %collective-permute-done.refs_1_ = bf16[4,160,640]{2,1,0:T(8,128)(2,1)S(1)} collective-permute-done((bf16[4,160,640]{2,1,0:T(8,128)(2,1)S(1)}, bf16[4,160,640]{2,1,0:T(8,128)(2,1)S(1)}, u32[]{:S(2)}, u32[]{:S(2)}) %collective-permute-start) | collective-permute-done | bytes 819232 | tf_op jit(solution)/shard_map/ppermute | solution.py:452
  31.2 2.5 %shard_map.104 = (bf16[2,160,1024]{2,1,0:T(8,128)(2,1)}, bf16[2,160,1024]{2,1,0:T(8,128)(2,1)S(1)}) custom-call(bf16[4,160,640]{2,1,0:T(8,128)(2,1)S(1)} %copy-done.5, bf16[4,160,640]{2,1,0:T(8,128)(2,1)S(1)} %collective-permute-done.refs_1_, bf16[960,512]{1,0:T(8,128)(2,1)S(1)} %copy-done.4, bf16[960,512]{1,0:T(8,128)(2,1)S(1)} %collective-permute-done.1.refs_3_), custom_call_target="tpu_custom_call" | custom-call | flops 1 | bytes 1 | tf_op jit(solution)/shard_map/pallas_call | solution.py:284
  33.7 2.8 %collective-permute-start.2 = (bf16[2,160,1024]{2,1,0:T(8,128)(2,1)}, bf16[2,160,1024]{2,1,0:T(8,128)(2,1)S(1)}, u32[]{:S(2)}, u32[]{:S(2)}) collective-permute-start(bf16[2,160,1024]{2,1,0:T(8,128)(2,1)} %get-tuple-element.53), channel_id=1, source_target_pairs={{0,8},{4,12},{8,0},{12,4},{16,24},{20,28},{24,16},{28,20},{1,9},{5... | collective-permute-start | bytes 1966088 | tf_op jit(solution)/shard_map/ppermute | solution.py:452
  36.5 1.6 %shard_map.105 = (bf16[2,160,896]{2,1,0:T(8,128)(2,1)S(1)}, bf16[2,160,896]{2,1,0:T(8,128)(2,1)S(1)}) custom-call(bf16[4,160,512]{2,1,0:T(8,128)(2,1)S(1)} %copy-done.1, bf16[4,160,512]{2,1,0:T(8,128)(2,1)S(1)} %collective-permute-done.3.refs_1_, bf16[960,512]{1,0:T(8,128)(2,1)S(1)} %copy-done, bf16[960,512]{1,0:T(8,128)(2,1)S(1)} %collective-permute-done.4.refs_3_.refs_5_), custom_call_target="tpu_custom_call" | custom-call | flops 1 | bytes 1 | tf_op jit(solution)/shard_map/pallas_call | solution.py:284
  38.1 1.6 %collective-permute-start.6 = (bf16[2,160,896]{2,1,0:T(8,128)(2,1)S(1)}, bf16[2,160,896]{2,1,0:T(8,128)(2,1)S(1)}, u32[]{:S(2)}, u32[]{:S(2)}) collective-permute-start(bf16[2,160,896]{2,1,0:T(8,128)(2,1)S(1)} %get-tuple-element.62), channel_id=1, source_target_pairs={{0,16},{4,20},{8,24},{12,28},{16,0},{20,4},{24,8},{28,12},{1,17},{... | collective-permute-start | bytes 1720328 | tf_op jit(solution)/shard_map/ppermute | solution.py:452
  39.7 6.4 %shard_map.106 = (bf16[960,512]{1,0:T(8,128)(2,1)}, bf16[960,512]{1,0:T(8,128)(2,1)}) custom-call(bf16[4,3,3,320,128]{4,3,2,1,0:T(8,128)(2,1)} %bitcast.70, bf16[4,12,128,128]{3,2,1,0:T(8,128)(2,1)} %get-tuple-element.59.refs_1_.refs_4_, bf16[4,960,128]{2,1,0:T(8,128)(2,1)} %get-tuple-element.50.refs_2_.refs_5_, bf16[4,3,3,320,128]{4,3,2,1,0:T(8,128)(2,1)} %bitcast.71, ...), custom_call_target="tpu_custom_call" | custom-call | flops 1 | bytes 1 | tf_op jit(solution)/shard_map/pallas_call | solution.py:426
  46.1 6.8 %collective-permute-done.6 = bf16[2,160,896]{2,1,0:T(8,128)(2,1)S(1)} collective-permute-done((bf16[2,160,896]{2,1,0:T(8,128)(2,1)S(1)}, bf16[2,160,896]{2,1,0:T(8,128)(2,1)S(1)}, u32[]{:S(2)}, u32[]{:S(2)}) %collective-permute-start.6) | collective-permute-done | bytes 573472 | tf_op jit(solution)/shard_map/ppermute | solution.py:452
  54.3 1.5 %collective-permute-start.5 = (bf16[160,1024]{1,0:T(8,128)(2,1)}, bf16[160,1024]{1,0:T(8,128)(2,1)}, u32[]{:S(2)}, u32[]{:S(2)}) collective-permute-start(bf16[160,1024]{1,0:T(8,128)(2,1)} %fusion.4), channel_id=1, source_target_pairs={{0,16},{4,20},{8,24},{12,28},{16,0},{20,4},{24,8},{28,12},{1,17},{... | collective-permute-start | bytes 983048 | tf_op jit(solution)/shard_map/ppermute | solution.py:328
  58.4 2.8 %shard_map.107 = (bf16[2,160,1024]{2,1,0:T(8,128)(2,1)S(1)}, bf16[2,160,1024]{2,1,0:T(8,128)(2,1)S(1)}) custom-call(bf16[4,160,512]{2,1,0:T(8,128)(2,1)S(1)} %copy-done.1, bf16[4,160,512]{2,1,0:T(8,128)(2,1)S(1)} %collective-permute-done.3.refs_1_, bf16[960,512]{1,0:T(8,128)(2,1)S(1)} %copy-done.2, bf16[960,512]{1,0:T(8,128)(2,1)S(1)} %copy-done, ...), custom_call_target="tpu_custom_call" | custom-call | flops 1 | bytes 1 | tf_op jit(solution)/shard_map/pallas_call | solution.py:284
  61.3 2.9 %shard_map.108 = (bf16[2,160,960]{2,1,0:T(8,128)(2,1)S(1)}, bf16[2,160,960]{2,1,0:T(8,128)(2,1)S(1)}) custom-call(bf16[4,160,512]{2,1,0:T(8,128)(2,1)S(1)} %copy-done.1, bf16[4,160,512]{2,1,0:T(8,128)(2,1)S(1)} %collective-permute-done.3.refs_1_, bf16[960,512]{1,0:T(8,128)(2,1)S(1)} %copy-done.3, bf16[960,512]{1,0:T(8,128)(2,1)} %collective-permute-done.8.refs_3_), custom_call_target="tpu_custom_call" | custom-call | flops 1 | bytes 1 | tf_op jit(solution)/shard_map/pallas_call | solution.py:284
  64.2 1.3 %collective-permute-done.7 = bf16[160,896]{1,0:T(8,128)(2,1)} collective-permute-done((bf16[160,896]{1,0:T(8,128)(2,1)}, bf16[160,896]{1,0:T(8,128)(2,1)}, u32[]{:S(2)}, u32[]{:S(2)}) %collective-permute-start.7) | collective-permute-done | bytes 286752 | tf_op jit(solution)/shard_map/ppermute | solution.py:328
  67.8 1.6 %collective-permute-start.14 = (bf16[40,1920]{1,0:T(8,128)(2,1)S(1)}, bf16[40,1920]{1,0:T(8,128)(2,1)S(1)}, u32[]{:S(2)}, u32[]{:S(2)}) collective-permute-start(bf16[40,1920]{1,0:T(8,128)(2,1)S(1)} %pad_maximum_fusion.4), channel_id=1, source_target_pairs={{0,1},{1,2},{2,3},{3,0},{4,5},{5,6},{6,7},{7,4},{8,9},{9,10},{10,1... | collective-permute-start | bytes 460808 | tf_op jit(solution)/shard_map/ppermute | solution.py:348
  70.5 2.7 %collective-permute-start.15 = (bf16[40,1920]{1,0:T(8,128)(2,1)S(1)}, bf16[40,1920]{1,0:T(8,128)(2,1)S(1)}, u32[]{:S(2)}, u32[]{:S(2)}) collective-permute-start(bf16[40,1920]{1,0:T(8,128)(2,1)S(1)} %pad_maximum_fusion.5), channel_id=1, source_target_pairs={{0,2},{1,3},{2,0},{3,1},{4,6},{5,7},{6,4},{7,5},{8,10},{9,11},{10,... | collective-permute-start | bytes 460808 | tf_op jit(solution)/shard_map/ppermute | solution.py:348
  73.2 1.4 %collective-permute-start.16 = (bf16[40,1920]{1,0:T(8,128)(2,1)S(1)}, bf16[40,1920]{1,0:T(8,128)(2,1)S(1)}, u32[]{:S(2)}, u32[]{:S(2)}) collective-permute-start(bf16[40,1920]{1,0:T(8,128)(2,1)S(1)} %pad_maximum_fusion.6), channel_id=1, source_target_pairs={{0,3},{1,0},{2,1},{3,2},{4,7},{5,4},{6,5},{7,6},{8,11},{9,8},{10,9... | collective-permute-start | bytes 460808 | tf_op jit(solution)/shard_map/ppermute | solution.py:348
  74.6 10.1 %collective-permute-done.11 = bf16[2,160,1024]{2,1,0:T(8,128)(2,1)S(1)} collective-permute-done((bf16[2,160,1024]{2,1,0:T(8,128)(2,1)S(1)}, bf16[2,160,1024]{2,1,0:T(8,128)(2,1)S(1)}, u32[]{:S(2)}, u32[]{:S(2)}) %collective-permute-start.11) | collective-permute-done | bytes 655392 | tf_op jit(solution)/shard_map/ppermute | solution.py:452
  86.0 1.4 %collective-permute-start.12 = (bf16[160,960]{1,0:T(8,128)(2,1)S(1)}, bf16[160,960]{1,0:T(8,128)(2,1)S(1)}, u32[]{:S(2)}, u32[]{:S(2)}) collective-permute-start(bf16[160,960]{1,0:T(8,128)(2,1)S(1)} %fusion.6), channel_id=1, source_target_pairs={{0,8},{4,12},{8,0},{12,4},{16,24},{20,28},{24,16},{28,20},{1,9},{5... | collective-permute-start | bytes 921608 | tf_op jit(solution)/shard_map/ppermute | solution.py:328
  87.6 5.2 %collective-permute-done.13 = bf16[160,1024]{1,0:T(8,128)(2,1)S(1)} collective-permute-done((bf16[160,1024]{1,0:T(8,128)(2,1)S(1)}, bf16[160,1024]{1,0:T(8,128)(2,1)S(1)}, u32[]{:S(2)}, u32[]{:S(2)}) %collective-permute-start.13) | collective-permute-done | bytes 327712 | tf_op jit(solution)/shard_map/ppermute | solution.py:328
  93.4 1.6 %collective-permute-start.17 = (bf16[40,1984]{1,0:T(8,128)(2,1)S(1)}, bf16[40,1984]{1,0:T(8,128)(2,1)S(1)}, u32[]{:S(2)}, u32[]{:S(2)}) collective-permute-start(bf16[40,1984]{1,0:T(8,128)(2,1)S(1)} %pad_maximum_fusion), channel_id=1, source_target_pairs={{0,1},{1,2},{2,3},{3,0},{4,5},{5,6},{6,7},{7,4},{8,9},{9,10},{10,1... | collective-permute-start | bytes 476168 | tf_op jit(solution)/shard_map/ppermute | solution.py:348
  95.1 1.6 %collective-permute-start.18 = (bf16[40,1984]{1,0:T(8,128)(2,1)S(1)}, bf16[40,1984]{1,0:T(8,128)(2,1)S(1)}, u32[]{:S(2)}, u32[]{:S(2)}) collective-permute-start(bf16[40,1984]{1,0:T(8,128)(2,1)S(1)} %pad_maximum_fusion.1), channel_id=1, source_target_pairs={{0,2},{1,3},{2,0},{3,1},{4,6},{5,7},{6,4},{7,5},{8,10},{9,11},{10,... | collective-permute-start | bytes 476168 | tf_op jit(solution)/shard_map/ppermute | solution.py:348
  96.7 2.4 %collective-permute-start.19 = (bf16[40,1984]{1,0:T(8,128)(2,1)S(1)}, bf16[40,1984]{1,0:T(8,128)(2,1)S(1)}, u32[]{:S(2)}, u32[]{:S(2)}) collective-permute-start(bf16[40,1984]{1,0:T(8,128)(2,1)S(1)} %pad_maximum_fusion.2), channel_id=1, source_target_pairs={{0,3},{1,0},{2,1},{3,2},{4,7},{5,4},{6,5},{7,6},{8,11},{9,8},{10,9... | collective-permute-start | bytes 476168 | tf_op jit(solution)/shard_map/ppermute | solution.py:348
  101.7 4.6 %collective-permute-done.18 = bf16[40,1984]{1,0:T(8,128)(2,1)S(1)} collective-permute-done((bf16[40,1984]{1,0:T(8,128)(2,1)S(1)}, bf16[40,1984]{1,0:T(8,128)(2,1)S(1)}, u32[]{:S(2)}, u32[]{:S(2)}) %collective-permute-start.18) | collective-permute-done | bytes 158752 | tf_op jit(solution)/shard_map/ppermute | solution.py:348
  (85 shorter events, 14.2 us)
Async XLA Ops:
  21.3 6.1 %collective-permute-start.1 = (bf16[960,512]{1,0:T(8,128)(2,1)}, bf16[960,512]{1,0:T(8,128)(2,1)S(1)}, u32[]{:S(2)}, u32[]{:S(2)}) collective-permute-start(bf16[960,512]{1,0:T(8,128)(2,1)} %get-tuple-element.47.refs_2_), channel_id=1, source_target_pairs={{0,4},{4,0},{8,12},{12,8},{16,20},{20,16},{24,28},{28,24},{1,5},{5... | collective-permute-start | bytes 2949128 | tf_op jit(solution)/shard_map/ppermute | solution.py:452
  21.8 9.3 %copy-start.5 = (bf16[4,160,640]{2,1,0:T(8,128)(2,1)S(1)}, bf16[4,160,640]{2,1,0:T(8,128)(2,1)}, u32[]{:S(2)}) copy-start(bf16[4,160,640]{2,1,0:T(8,128)(2,1)} %get-tuple-element.45.refs_0_) | copy-start | bytes 2457604
  26.8 9.7 %collective-permute-start.4 = (bf16[960,512]{1,0:T(8,128)(2,1)}, bf16[960,512]{1,0:T(8,128)(2,1)S(1)}, u32[]{:S(2)}, u32[]{:S(2)}) collective-permute-start(bf16[960,512]{1,0:T(8,128)(2,1)} %shard_map.103.refs_2_.refs_3_), channel_id=1, source_target_pairs={{0,4},{4,0},{8,12},{12,8},{16,20},{20,16},{24,28},{28,24},{1,5},{5... | collective-permute-start | bytes 2949128 | tf_op jit(solution)/shard_map/ppermute | solution.py:452
  26.8 4.3 %collective-permute-start = (bf16[4,160,640]{2,1,0:T(8,128)(2,1)S(1)}, bf16[4,160,640]{2,1,0:T(8,128)(2,1)S(1)}, u32[]{:S(2)}, u32[]{:S(2)}) collective-permute-start(bf16[4,160,640]{2,1,0:T(8,128)(2,1)S(1)} %copy-done.15), channel_id=1, source_target_pairs={{0,4},{4,0},{8,12},{12,8},{16,20},{20,16},{24,28},{28,24},{1,5},{5... | collective-permute-start | bytes 2457608 | tf_op jit(solution)/shard_map/ppermute | solution.py:452
  27.3 9.2 %collective-permute-start.3 = (bf16[4,160,512]{2,1,0:T(8,128)(2,1)}, bf16[4,160,512]{2,1,0:T(8,128)(2,1)S(1)}, u32[]{:S(2)}, u32[]{:S(2)}) collective-permute-start(bf16[4,160,512]{2,1,0:T(8,128)(2,1)} %get-tuple-element.55), channel_id=1, source_target_pairs={{0,4},{4,0},{8,12},{12,8},{16,20},{20,16},{24,28},{28,24},{1,5},{5... | collective-permute-start | bytes 1966088 | tf_op jit(solution)/shard_map/ppermute | solution.py:452
  33.7 19.8 %copy-start.6 = (bf16[2,160,1024]{2,1,0:T(8,128)(2,1)}, bf16[2,160,1024]{2,1,0:T(8,128)(2,1)S(1)}, u32[]{:S(2)}) copy-start(bf16[2,160,1024]{2,1,0:T(8,128)(2,1)S(1)} %get-tuple-element.52) | copy-start | bytes 1966084
  33.7 19.2 %collective-permute-start.2 = (bf16[2,160,1024]{2,1,0:T(8,128)(2,1)}, bf16[2,160,1024]{2,1,0:T(8,128)(2,1)S(1)}, u32[]{:S(2)}, u32[]{:S(2)}) collective-permute-start(bf16[2,160,1024]{2,1,0:T(8,128)(2,1)} %get-tuple-element.53), channel_id=1, source_target_pairs={{0,8},{4,12},{8,0},{12,4},{16,24},{20,28},{24,16},{28,20},{1,9},{5... | collective-permute-start | bytes 1966088 | tf_op jit(solution)/shard_map/ppermute | solution.py:452
  38.1 17.8 %copy-start.8 = (bf16[2,160,896]{2,1,0:T(8,128)(2,1)}, bf16[2,160,896]{2,1,0:T(8,128)(2,1)S(1)}, u32[]{:S(2)}) copy-start(bf16[2,160,896]{2,1,0:T(8,128)(2,1)S(1)} %get-tuple-element.58) | copy-start | bytes 1720324
  38.1 14.8 %collective-permute-start.6 = (bf16[2,160,896]{2,1,0:T(8,128)(2,1)S(1)}, bf16[2,160,896]{2,1,0:T(8,128)(2,1)S(1)}, u32[]{:S(2)}, u32[]{:S(2)}) collective-permute-start(bf16[2,160,896]{2,1,0:T(8,128)(2,1)S(1)} %get-tuple-element.62), channel_id=1, source_target_pairs={{0,16},{4,20},{8,24},{12,28},{16,0},{20,4},{24,8},{28,12},{1,17},{... | collective-permute-start | bytes 1720328 | tf_op jit(solution)/shard_map/ppermute | solution.py:452
  52.9 4.3 %collective-permute-start.9 = (bf16[960,512]{1,0:T(8,128)(2,1)}, bf16[960,512]{1,0:T(8,128)(2,1)}, u32[]{:S(2)}, u32[]{:S(2)}) collective-permute-start(bf16[960,512]{1,0:T(8,128)(2,1)} %get-tuple-element.66.refs_2_), channel_id=1, source_target_pairs={{0,4},{4,0},{8,12},{12,8},{16,20},{20,16},{24,28},{28,24},{1,5},{5... | collective-permute-start | bytes 2949128 | tf_op jit(solution)/shard_map/ppermute | solution.py:452
  53.0 8.2 %collective-permute-start.8 = (bf16[960,512]{1,0:T(8,128)(2,1)}, bf16[960,512]{1,0:T(8,128)(2,1)}, u32[]{:S(2)}, u32[]{:S(2)}) collective-permute-start(bf16[960,512]{1,0:T(8,128)(2,1)} %get-tuple-element.65.refs_2_), channel_id=1, source_target_pairs={{0,4},{4,0},{8,12},{12,8},{16,20},{20,16},{24,28},{28,24},{1,5},{5... | collective-permute-start | bytes 2949128 | tf_op jit(solution)/shard_map/ppermute | solution.py:452
  54.3 11.2 %collective-permute-start.5 = (bf16[160,1024]{1,0:T(8,128)(2,1)}, bf16[160,1024]{1,0:T(8,128)(2,1)}, u32[]{:S(2)}, u32[]{:S(2)}) collective-permute-start(bf16[160,1024]{1,0:T(8,128)(2,1)} %fusion.4), channel_id=1, source_target_pairs={{0,16},{4,20},{8,24},{12,28},{16,0},{20,4},{24,8},{28,12},{1,17},{... | collective-permute-start | bytes 983048 | tf_op jit(solution)/shard_map/ppermute | solution.py:328
  56.6 8.9 %collective-permute-start.7 = (bf16[160,896]{1,0:T(8,128)(2,1)}, bf16[160,896]{1,0:T(8,128)(2,1)}, u32[]{:S(2)}, u32[]{:S(2)}) collective-permute-start(bf16[160,896]{1,0:T(8,128)(2,1)} %fusion.10), channel_id=1, source_target_pairs={{0,8},{4,12},{8,0},{12,4},{16,24},{20,28},{24,16},{28,20},{1,9},{5... | collective-permute-start | bytes 860168 | tf_op jit(solution)/shard_map/ppermute | solution.py:328
  67.8 19.7 %collective-permute-start.14 = (bf16[40,1920]{1,0:T(8,128)(2,1)S(1)}, bf16[40,1920]{1,0:T(8,128)(2,1)S(1)}, u32[]{:S(2)}, u32[]{:S(2)}) collective-permute-start(bf16[40,1920]{1,0:T(8,128)(2,1)S(1)} %pad_maximum_fusion.4), channel_id=1, source_target_pairs={{0,1},{1,2},{2,3},{3,0},{4,5},{5,6},{6,7},{7,4},{8,9},{9,10},{10,1... | collective-permute-start | bytes 460808 | tf_op jit(solution)/shard_map/ppermute | solution.py:348
  69.4 15.3 %collective-permute-start.11 = (bf16[2,160,1024]{2,1,0:T(8,128)(2,1)S(1)}, bf16[2,160,1024]{2,1,0:T(8,128)(2,1)S(1)}, u32[]{:S(2)}, u32[]{:S(2)}) collective-permute-start(bf16[2,160,1024]{2,1,0:T(8,128)(2,1)S(1)} %get-tuple-element.73), channel_id=1, source_target_pairs={{0,8},{4,12},{8,0},{12,4},{16,24},{20,28},{24,16},{28,20},{1,9},{5... | collective-permute-start | bytes 1966088 | tf_op jit(solution)/shard_map/ppermute | solution.py:452
  70.0 15.3 %collective-permute-start.10 = (bf16[2,160,960]{2,1,0:T(8,128)(2,1)S(1)}, bf16[2,160,960]{2,1,0:T(8,128)(2,1)S(1)}, u32[]{:S(2)}, u32[]{:S(2)}) collective-permute-start(bf16[2,160,960]{2,1,0:T(8,128)(2,1)S(1)} %get-tuple-element.72), channel_id=1, source_target_pairs={{0,16},{4,20},{8,24},{12,28},{16,0},{20,4},{24,8},{28,12},{1,17},{... | collective-permute-start | bytes 1843208 | tf_op jit(solution)/shard_map/ppermute | solution.py:452
  70.5 17.0 %collective-permute-start.15 = (bf16[40,1920]{1,0:T(8,128)(2,1)S(1)}, bf16[40,1920]{1,0:T(8,128)(2,1)S(1)}, u32[]{:S(2)}, u32[]{:S(2)}) collective-permute-start(bf16[40,1920]{1,0:T(8,128)(2,1)S(1)} %pad_maximum_fusion.5), channel_id=1, source_target_pairs={{0,2},{1,3},{2,0},{3,1},{4,6},{5,7},{6,4},{7,5},{8,10},{9,11},{10,... | collective-permute-start | bytes 460808 | tf_op jit(solution)/shard_map/ppermute | solution.py:348
  73.2 14.3 %collective-permute-start.16 = (bf16[40,1920]{1,0:T(8,128)(2,1)S(1)}, bf16[40,1920]{1,0:T(8,128)(2,1)S(1)}, u32[]{:S(2)}, u32[]{:S(2)}) collective-permute-start(bf16[40,1920]{1,0:T(8,128)(2,1)S(1)} %pad_maximum_fusion.6), channel_id=1, source_target_pairs={{0,3},{1,0},{2,1},{3,2},{4,7},{5,4},{6,5},{7,6},{8,11},{9,8},{10,9... | collective-permute-start | bytes 460808 | tf_op jit(solution)/shard_map/ppermute | solution.py:348
  85.4 7.4 %collective-permute-start.13 = (bf16[160,1024]{1,0:T(8,128)(2,1)S(1)}, bf16[160,1024]{1,0:T(8,128)(2,1)S(1)}, u32[]{:S(2)}, u32[]{:S(2)}) collective-permute-start(bf16[160,1024]{1,0:T(8,128)(2,1)S(1)} %fusion.7), channel_id=1, source_target_pairs={{0,16},{4,20},{8,24},{12,28},{16,0},{20,4},{24,8},{28,12},{1,17},{... | collective-permute-start | bytes 983048 | tf_op jit(solution)/shard_map/ppermute | solution.py:328
  86.0 7.1 %collective-permute-start.12 = (bf16[160,960]{1,0:T(8,128)(2,1)S(1)}, bf16[160,960]{1,0:T(8,128)(2,1)S(1)}, u32[]{:S(2)}, u32[]{:S(2)}) collective-permute-start(bf16[160,960]{1,0:T(8,128)(2,1)S(1)} %fusion.6), channel_id=1, source_target_pairs={{0,8},{4,12},{8,0},{12,4},{16,24},{20,28},{24,16},{28,20},{1,9},{5... | collective-permute-start | bytes 921608 | tf_op jit(solution)/shard_map/ppermute | solution.py:328
  87.6 12.3 %copy-start.10 = (f32[40,1920]{1,0:T(8,128)}, f32[40,1920]{1,0:T(8,128)S(1)}, u32[]{:S(2)}) copy-start(f32[40,1920]{1,0:T(8,128)S(1)} %convert_add_fusion.5) | copy-start | bytes 921604
  93.4 8.3 %collective-permute-start.17 = (bf16[40,1984]{1,0:T(8,128)(2,1)S(1)}, bf16[40,1984]{1,0:T(8,128)(2,1)S(1)}, u32[]{:S(2)}, u32[]{:S(2)}) collective-permute-start(bf16[40,1984]{1,0:T(8,128)(2,1)S(1)} %pad_maximum_fusion), channel_id=1, source_target_pairs={{0,1},{1,2},{2,3},{3,0},{4,5},{5,6},{6,7},{7,4},{8,9},{9,10},{10,1... | collective-permute-start | bytes 476168 | tf_op jit(solution)/shard_map/ppermute | solution.py:348
  95.1 11.3 %collective-permute-start.18 = (bf16[40,1984]{1,0:T(8,128)(2,1)S(1)}, bf16[40,1984]{1,0:T(8,128)(2,1)S(1)}, u32[]{:S(2)}, u32[]{:S(2)}) collective-permute-start(bf16[40,1984]{1,0:T(8,128)(2,1)S(1)} %pad_maximum_fusion.1), channel_id=1, source_target_pairs={{0,2},{1,3},{2,0},{3,1},{4,6},{5,7},{6,4},{7,5},{8,10},{9,11},{10,... | collective-permute-start | bytes 476168 | tf_op jit(solution)/shard_map/ppermute | solution.py:348
  96.7 9.6 %collective-permute-start.19 = (bf16[40,1984]{1,0:T(8,128)(2,1)S(1)}, bf16[40,1984]{1,0:T(8,128)(2,1)S(1)}, u32[]{:S(2)}, u32[]{:S(2)}) collective-permute-start(bf16[40,1984]{1,0:T(8,128)(2,1)S(1)} %pad_maximum_fusion.2), channel_id=1, source_target_pairs={{0,3},{1,0},{2,1},{3,2},{4,7},{5,4},{6,5},{7,6},{8,11},{9,8},{10,9... | collective-permute-start | bytes 476168 | tf_op jit(solution)/shard_map/ppermute | solution.py:348
  (13 other events, 61.8 us)

commit v2 on v1

--- a/solution.py
+++ b/solution.py
@@ -9,7 +9,6 @@
 
 HEADS = 12
 STAGE = 4
-PARTS = 3
 JOIN = 4
 PAIR = 2
 LANES = 128
@@ -167,7 +166,7 @@
         row_at = lax.broadcasted_iota(jnp.int32, (strip, 1), 0)
         alive = alive_of(row_at, live_ref[0, PAIR * pair], live_ref[0, PAIR * pair + 1], group)
         alive = jnp.where(alive, 1.0, 0.0)
-        gain = gain_ref[...]
+        gain = gain_ref[...].reshape(1, model_width)
         out_rows = pl.ds(pl.multiple_of(pair * strip, strip), strip)
         for turn in range(JOIN):
             here = pl.ds(pl.multiple_of(pair * block + turn * strip, strip), strip)
@@ -205,16 +204,28 @@
         outs[n].wait()
 
 
-def backward_kernel(*refs):
-    for packed_ref, probs_ref, d_context_ref, d_packed_ref in zip(*[iter(refs)] * 4):
-        _, heads, block, _ = probs_ref.shape
-        height = d_context_ref.shape[1]
-        head_width = height // heads
-        scale = head_width ** (-0.5)
-        spans = [slice(head * head_width, (head + 1) * head_width) for head in range(heads)]
-        probs = [probs_ref[0, head] for head in range(heads)]
+def backward_kernel(packed_ref, probs_ref, d_context_ref, *outs):
+    _, heads, block, _ = probs_ref.shape
+    inner = d_context_ref.shape[1]
+    head_width = inner // heads
+    scale = head_width ** (-0.5)
+
+    def put(at, value):
+        value = value.astype(BF16)
+        for ref in outs:
+            taken = max(0, min(ref.shape[0] - at, value.shape[0]))
+            if taken > 0:
+                ref[at:at + taken, :] = value[:taken]
+                value = value[taken:]
+                at += taken
+            at -= ref.shape[0]
+
+    for first in range(0, heads, STAGE):
+        together = range(first, first + STAGE)
+        spans = [slice(head * head_width, (head + 1) * head_width) for head in together]
+        probs = [probs_ref[0, head] for head in together]
         d_probs = [
-            dot(packed_ref[0, 2, 0, span, :], d_context_ref[0, span, :], 0, 0) for span in spans
+            dot(packed_ref[0, 2, span, :], d_context_ref[0, span, :], 0, 0) for span in spans
         ]
         d_scores = []
         for low, one in zip(probs, d_probs):
@@ -222,73 +233,67 @@
             inside = jnp.sum(one * exact, axis=0, keepdims=True)
             d_scores.append((exact * (one - inside) * scale).astype(BF16))
         founds = (
-            [dot(packed_ref[0, 1, 0, span, :], one) for span, one in zip(spans, d_scores)],
-            [dot(packed_ref[0, 0, 0, span, :], one, 1, 1) for span, one in zip(spans, d_scores)],
+            [dot(packed_ref[0, 1, span, :], one) for span, one in zip(spans, d_scores)],
+            [dot(packed_ref[0, 0, span, :], one, 1, 1) for span, one in zip(spans, d_scores)],
             [dot(d_context_ref[0, span, :], one, 1, 1) for span, one in zip(spans, probs)],
         )
         for n, found in enumerate(founds):
             for span, one in zip(spans, found):
-                d_packed_ref[n * height + span.start:n * height + span.stop, :] = one.astype(BF16)
-
-
-def product_kernel(*refs, taken, spans, extra_at):
-    keep_ref, other_ref = refs[:2]
-    rights = refs[2:-2]
-    outs = refs[-2:]
-    rank_rows, width = outs[0].shape[1:]
-    depth = rights[0].shape[1]
+                put(n * inner + span.start, one)
+
+
+def product_kernel(keep_ref, other_ref, right_ref, right_other_ref, *outs, pieces, extra_at):
+    half, rank_rows, _ = keep_ref.shape
+    depth = right_ref.shape[1]
     whole = rank_rows % 16 == 0
-    lists = [[(n, g) for g in places] for n, places in enumerate(taken)]
-    lists = [lists[0] + lists[1]] if whole else [[one] for one in lists[0] + lists[1]]
-    count = len(rights) // 2
-    sides = []
-    for side in range(2):
-        pieces = [
-            ref[first:last] for ref, (first, last) in zip(rights[side * count:], spans)
-        ]
-        sides.append(jnp.concatenate(pieces, axis=0) if count > 1 else pieces[0])
-    for ordered in lists:
+    for groups in [list(range(half))] if whole else [[g] for g in range(half)]:
         lefts = []
         for ref in (keep_ref, other_ref):
-            pieces = [ref[g] for _, g in ordered]
-            lefts.append(jnp.concatenate(pieces, axis=0) if whole else pieces[0])
-        for at, size in tiles(sides[0].shape[0], 2 * TILE):
-            total = dot(lefts[0][:, :depth], sides[0][at:at + size], 1, 1)
-            total += dot(lefts[1][:, :depth], sides[1][at:at + size], 1, 1)
-            place = [0, 0]
-            for n, (side, g) in enumerate(ordered):
-                spot = taken[side].index(g)
-                outs[side][spot, :, at:at + size] = total[
-                    n * rank_rows:(n + 1) * rank_rows
-                ].astype(BF16)
-        if extra_at is not None:
-            column = lax.broadcasted_iota(jnp.int32, (LANES, LANES), 1)
-            ones = jnp.where(column == extra_at % LANES, 1.0, 0.0).astype(BF16)
-            total = dot(lefts[0][:, depth:], ones) + dot(lefts[1][:, depth:], ones)
-            for n, (side, g) in enumerate(ordered):
-                spot = taken[side].index(g)
-                outs[side][spot, :, extra_at:] = total[
-                    n * rank_rows:(n + 1) * rank_rows, extra_at % LANES:
-                ].astype(BF16)
-
-
-def product(left, own, theirs, spans, bit, extra_at=None):
+            rows = [ref[g] for g in groups]
+            lefts.append(jnp.concatenate(rows, axis=0) if whole else rows[0])
+        number = 0
+        for (first, last), lists in pieces:
+            def put(total, at):
+                for n, g in enumerate(groups):
+                    for ref, held in zip(outs[number:], lists):
+                        if g in held:
+                            ref[held.index(g), :, at:at + total.shape[1]] = total[
+                                n * rank_rows:(n + 1) * rank_rows
+                            ].astype(BF16)
+
+            for at, size in tiles(last - first, 2 * TILE):
+                span = slice(first + at, first + at + size)
+                total = dot(lefts[0][:, :depth], right_ref[span, :], 1, 1)
+                total += dot(lefts[1][:, :depth], right_other_ref[span, :], 1, 1)
+                put(total, at)
+            if extra_at is not None:
+                column = lax.broadcasted_iota(jnp.int32, (LANES, LANES), 1)
+                ones = jnp.where(column == extra_at % LANES, 1.0, 0.0).astype(BF16)
+                total = dot(lefts[0][:, depth:], ones) + dot(lefts[1][:, depth:], ones)
+                put(total[:, extra_at % LANES:], extra_at)
+            number += len(lists)
+
+
+def product(left, right, pieces, extra_at=None):
     keep, other = left
     half, rank_rows, _ = keep.shape
-    depth = own[0].shape[1]
-    columns = sum(last - first for first, last in spans)
-    width = columns if extra_at is None else ceil_to(columns + 1, LANES)
-    sent = [g for g in range(half) if (g >> (bit - 1)) & 1]
-    kept = [g for g in range(half) if g not in sent]
-    shape = jax.ShapeDtypeStruct((half // 2, rank_rows, width), BF16)
-    return pl.pallas_call(
-        functools.partial(product_kernel, taken=(sent, kept), spans=spans, extra_at=extra_at),
-        out_shape=[shape, shape],
-        in_specs=[VMEM] * (2 + 2 * len(own)),
-        out_specs=[VMEM] * 2,
-        compiler_params=pltpu.CompilerParams(vmem_limit_bytes=20 * 2**20),
+    taken, shapes, counts = [], [], []
+    for (first, last), axis in pieces:
+        sent = [] if axis == "vis" else [g for g in range(half) if (g >> (axis - 1)) & 1]
+        lists = [held for held in (sent, [g for g in range(half) if g not in sent]) if held]
+        width = last - first if extra_at is None else ceil_to(last - first + 1, LANES)
+        taken.append(((first, last), lists))
+        shapes += [jax.ShapeDtypeStruct((len(held), rank_rows, width), BF16) for held in lists]
+        counts.append(len(lists))
+    found = pl.pallas_call(
+        functools.partial(product_kernel, pieces=taken, extra_at=extra_at),
+        out_shape=shapes,
+        in_specs=[VMEM] * 4,
+        out_specs=[VMEM] * len(shapes),
+        compiler_params=pltpu.CompilerParams(vmem_limit_bytes=24 * 2**20),
         cost_estimate=SMALL,
-    )(keep, other, *own, *theirs)
+    )(keep, other, *right)
+    return [found[sum(counts[:n]):sum(counts[:n + 1])] for n in range(len(counts))]
 
 
 def flip_pairs(size, bit):
@@ -299,40 +304,75 @@
     return lax.dynamic_index_in_dim(array, place, axis, keepdims=False)
 
 
-def add_low(first, second):
-    return (first.astype(F32) + second.astype(F32)).astype(BF16)
+def together(arrays, others):
+    found = lax.optimization_barrier((*arrays, *others))
+    return list(found[:len(arrays)]), list(found[len(arrays):])
 
 
 class Sum:
-    def __init__(self, kept, got, order):
-        self.ranks, self.layers = lax.axis_size("dp"), lax.axis_size("vis")
-        self.order = order[1:]
-        self.left = [b for b in range(len(order), 0, -1) if b != order[0]]
+    def __init__(self, kept, order):
+        self.ranks = lax.axis_size("dp")
+        self.order = list(order)
+        self.left = [b for b in range(self.ranks.bit_length() - 2, 0, -1)]
+        self.kept, self.got = kept, []
+
+    def first(self, sent, kept):
+        self.arrived(lax.ppermute(sent, "dp", flip_pairs(self.ranks, self.order[0])), kept)
+
+    def arrived(self, got, kept):
+        bit, *self.order = self.order
+        self.left.remove(bit)
         shape = (2,) * len(self.left) + kept.shape[1:]
         self.kept, self.got = kept.reshape(shape), [got.reshape(shape)]
 
-    def after(self, other):
-        *self.got, other = lax.optimization_barrier((*self.got, other))
-        return other
+    def after(self, others):
+        self.got, others = together(self.got, others)
+        return others
 
     def step(self):
-        got = self.got[0]
-        if self.order:
-            bit, *self.order = self.order
-            axis = self.left.index(bit)
-            halves = [
-                [lax.index_in_dim(array, n, axis, keepdims=False) for n in range(2)]
-                for array in (self.kept, got)
-            ]
-            sent = add_low(halves[0][1], halves[1][1])
-            self.got = [lax.ppermute(sent, "dp", flip_pairs(self.ranks, bit))]
-            self.kept = add_low(halves[0][0], halves[1][0])
-            self.left.remove(bit)
+        axis, *self.order = self.order
+        terms = [self.kept, *self.got]
+        if axis == "vis":
+            layers, layer = lax.axis_size("vis"), lax.axis_index("vis")
+            whole = total_of(terms).astype(BF16)
+            places = 2 ** len(self.left)
+            shards = whole.reshape(places, layers, -1, whole.shape[-1])
+            self.kept = pick(shards, layer, 1)
+            self.got = []
+            for k in range(1, layers):
+                pairs = [(i, (i + k) % layers) for i in range(layers)]
+                sent = pick(shards, (layer + k) % layers, 1)
+                self.got.append(lax.ppermute(sent, "vis", pairs))
             return
-        self.kept, self.got = add_low(self.kept, got), []
-
-
-class Spread:
+        sent = self.part(axis)
+        self.got = [lax.ppermute(sent, "dp", flip_pairs(self.ranks, axis))]
+
+    def part(self, axis):
+        shape = (2,) * len(self.left) + self.kept.shape[-2:]
+        at = self.left.index(axis)
+        terms = [one.reshape(shape) for one in (self.kept, *self.got)]
+        self.kept, sent = [
+            total_of([lax.index_in_dim(one, n, at, keepdims=False) for one in terms]).astype(BF16)
+            for n in range(2)
+        ]
+        self.left.remove(axis)
+        return sent
+
+    def total(self):
+        return total_of([self.kept, *self.got])
+
+    def whole(self):
+        return self.total().astype(BF16).reshape(self.kept.shape[-2:])
+
+
+def total_of(terms):
+    total = terms[0].astype(F32)
+    for one in terms[1:]:
+        total = total + one.astype(F32)
+    return total
+
+
+class Spread(Sum):
     def __init__(self, wholes):
         layers, layer = lax.axis_size("vis"), lax.axis_index("vis")
         shards = [whole.reshape(layers, -1, whole.shape[-1]) for whole in wholes]
@@ -346,12 +386,6 @@
         for k in range(1, layers):
             pairs = [(i, (i + k) % layers) for i in range(layers)]
             self.got.append(lax.ppermute(row_of(k), "vis", pairs))
-
-    def total(self):
-        total = self.kept.astype(F32)
-        for one in self.got:
-            total = total + one.astype(F32)
-        return total
 
 
 VMEM = pl.BlockSpec(memory_space=pltpu.VMEM)
@@ -405,33 +439,21 @@
     )(rank, window_live, window_index, patches, gain, d_merged, w_qkv, w_out)
 
 
-def run_backward(packed, probs, d_context, taken):
+def run_backward(packed, probs, d_context, heights):
     pairs, _, inner, block = packed.shape
-    heads, height = HEADS // PARTS, inner // PARTS
-
-    def specs(part):
-        return [
-            pl.BlockSpec((1, 3, 1, height, block), lambda n: (n, 0, part, 0, 0)),
-            pl.BlockSpec((1, heads, block, block), lambda n: (n, part, 0, 0)),
-            pl.BlockSpec((1, height, block), lambda n: (n, part, 0)),
-        ]
-
-    def body(*refs):
-        ins, outs = refs[:3 * len(taken)], refs[3 * len(taken):]
-        backward_kernel(*[
-            ref for n in range(len(taken)) for ref in (*ins[3 * n:3 * n + 3], outs[n])
-        ])
-
-    packed = packed.reshape(pairs, 3, PARTS, height, block)
     return pl.pallas_call(
-        body,
-        out_shape=[jax.ShapeDtypeStruct((3 * height, pairs * block), BF16) for _ in taken],
+        backward_kernel,
+        out_shape=[jax.ShapeDtypeStruct((h, pairs * block), BF16) for h in heights],
         grid=(pairs,),
-        in_specs=[spec for part in taken for spec in specs(part)],
-        out_specs=[pl.BlockSpec((3 * height, block), lambda n: (0, n)) for _ in taken],
+        in_specs=[
+            pl.BlockSpec((1, 3, inner, block), lambda n: (n, 0, 0, 0)),
+            pl.BlockSpec((1, HEADS, block, block), lambda n: (n, 0, 0, 0)),
+            pl.BlockSpec((1, inner, block), lambda n: (n, 0, 0)),
+        ],
+        out_specs=[pl.BlockSpec((h, block), lambda n: (0, n)) for h in heights],
         compiler_params=pltpu.CompilerParams(vmem_limit_bytes=56 * 2**20),
         cost_estimate=SMALL,
-    )(*[packed, probs, d_context] * len(taken))
+    )(packed, probs, d_context)
 
 
 def on_device(patches, window_index, window_live, d_merged, w_qkv, w_out, merge_gain):
@@ -440,89 +462,64 @@
     ranks = lax.axis_size("dp")
     rank = lax.axis_index("dp")
     bits = ranks.bit_length() - 2
-    after = lax.optimization_barrier
     (
         merged, packed, probs, d_context, context, norm_keep, norm_send, att_keep, att_send
     ) = run_forward(
         rank.reshape(1), window_live, window_index, patches,
-        merge_gain.reshape(1, model_width), d_merged, w_qkv.T, w_out, ranks // 2,
-    )
-
-    def swap(array, bit=0):
-        return lax.ppermute(array, "dp", flip_pairs(ranks, bit))
+        merge_gain, d_merged, w_qkv.T, w_out, ranks // 2,
+    )
+
+    def swap(array):
+        return lax.ppermute(array, "dp", flip_pairs(ranks, 0))
 
     along = list(range(1, bits + 1))
-    by_x = along
-    by_y = along[bits // 2:] + along[:bits // 2]
-    height = inner // PARTS
-    rest = 3 * height % LANES
-    full = 3 * height - rest
-
-    att_got, context_got, norm_got = swap(att_send), swap(context), swap(norm_send)
-    (d_first,) = run_backward(packed, probs, d_context, (0,))
+    by_x = along + ["vis"]
+    by_y = along[bits // 2:] + along[:bits // 2] + ["vis"]
+    early, late, last = 8 * LANES, 15 * LANES, 3 * inner
+
+    got = [swap(context), swap(att_send), swap(norm_send)]
+    d_first, d_last = run_backward(packed, probs, d_context, (early, last - early))
+    got, (d_first, d_last) = together(got, [d_first, d_last])
+    context_got, att_got, norm_got = got
     first_got = swap(d_first)
-
-    context_got, d_first = after((context_got, d_first))
-    sent, kept_out = product(
-        (att_keep, att_got), [context], [context_got], [(0, inner)], by_x[0], inner
-    )
-    sum_out = Sum(kept_out, swap(sent, by_x[0]), by_x)
-
-    first_got, kept_out = after((first_got, kept_out))
     norm = (norm_keep, norm_got)
-    sent, kept_1 = product(norm, [d_first], [first_got], [(0, full)], by_y[0])
-    sum_1 = Sum(kept_1, swap(sent, by_y[0]), by_y)
-
-    probs, kept_1 = after((probs, kept_1))
-    d_second, d_third = run_backward(packed, probs, d_context, (1, 2))
-    d_second = sum_out.after(d_second)
-    second_got = swap(d_second)
-    d_third = sum_1.after(d_third)
-    third_got = swap(d_third)
-
-    sum_out.step()
-    sent, kept_2 = product(
-        norm, [d_second, d_first], [second_got, first_got],
-        [(0, 3 * height), (full, 3 * height)], by_x[0],
-    )
-    sum_2 = Sum(kept_2, swap(sent, by_x[0]), by_x)
-
-    sum_1.step()
-    third_got, kept_2 = after((third_got, kept_2))
-    sent, kept_3 = product(norm, [d_third], [third_got], [(0, 3 * height)], by_y[0])
-    kept_3 = sum_1.after(kept_3)
-    kept_3 = sum_out.after(kept_3)
-    sum_3 = Sum(kept_3, swap(sent, by_y[0]), by_y)
-
-    for _ in range(bits - 2):
-        for one in (sum_out, sum_1, sum_2, sum_3):
-            one.step()
-    sum_out.step()
-    sum_1.step()
-    early = Spread([sum_out.kept, sum_1.kept])
-    early.kept = sum_2.after(early.kept)
-    sum_2.step()
-    early.kept = sum_3.after(early.kept)
-    sum_3.step()
-    total = early.total()
-    total = sum_2.after(total)
-    total = sum_3.after(total)
-    sum_2.step()
-    sum_3.step()
-    width = sum_out.kept.shape[-1]
+
+    ((sent, kept),) = product(
+        (att_keep, att_got), (context, context_got), [((0, inner), by_x[0])], inner
+    )
+    sum_out = Sum(None, by_x)
+    sum_out.first(sent, kept)
+
+    (first_got,), (d_last, sum_out.kept) = together([first_got], [d_last, sum_out.kept])
+    last_got = swap(d_last)
+    ((sent, kept),) = product(norm, (d_first, first_got), [((0, early), by_y[0])])
+    sum_1 = Sum(None, by_y)
+    sum_1.first(sent, kept)
+
+    (last_got,), (sum_1.kept,) = together([last_got], [sum_1.kept])
+    (sent_2, kept_2), (sent_3, kept_3) = product(
+        norm, (d_last, last_got), [((0, late - early), by_x[0]), ((late - early, last - early), by_y[0])]
+    )
+
+    kept_2, sent_2 = sum_out.after([kept_2, sent_2])
+    kept_3, sent_3 = sum_1.after([kept_3, sent_3])
+    sum_2, sum_3 = Sum(None, by_x), Sum(None, by_y)
+    sum_2.first(sent_2, kept_2)
+    sum_3.first(sent_3, kept_3)
+    for _ in range(bits - 1):
+        sum_out.step()
+        sum_1.step()
+    spread_1 = Spread([sum_out.whole(), sum_1.whole()])
+    for _ in range(bits - 1):
+        sum_2.step()
+        sum_3.step()
+    wholes = [sum_2.whole(), sum_3.whole()]
+    spread_1.got, wholes = together(spread_1.got, wholes)
+    spread_2 = Spread(wholes)
+    total, total_late = spread_1.total(), spread_2.total()
+    width = ceil_to(inner + 1, LANES)
     total_out, total_1 = total[:, :width], total[:, width:]
-    total = Spread([sum_2.kept, sum_3.kept]).total()
-    width = sum_2.kept.shape[-1]
-    total_2, total_3 = total[:, :width], total[:, width:]
-
-    columns = []
-    for part in range(3):
-        at = part * height
-        columns.append(total_1[:, at:min(at + height, full)])
-        if part == 2 and rest:
-            columns.append(total_2[:, 3 * height:])
-        columns += [total_2[:, at:at + height], total_3[:, at:at + height]]
-    total_qkv = jnp.concatenate(columns, axis=-1)
+    total_qkv = jnp.concatenate([total_1, total_late], axis=-1)
     return (merged, total_qkv, total_out[:, :inner].T, total_out[:, inner])
 
 

time: 108 us -> 99.8 us (0.924)
  Pallas kernels: 40.5 us -> 33.6 us
  local copies, waits for them, and re-layouts: 5.25 us -> 1.53 us
  other arithmetic: 4.58 us -> 7.48 us
    pallas_call x6 -> x4, Pallas kernels: 21.1 us -> 14.1 us  [the longest x1 8 us: run_backward(): pl.pallas_call(backward_kernel, out_shape=[jax.ShapeDtypeStruct((h, pairs...]
    convert_element_type x8, other arithmetic: 4.32 us -> 6.43 us  [the longest x4 3.8 us: part(): total_of([lax.index_in_dim(one, n, at, keepdims=False) for one in terms])]
    ppermute x14 -> x13, starting transfers between devices: 11.3 us -> 12.7 us  [the longest x4 5.95 us: first(): lax.ppermute(sent, 'dp', flip_pairs(self.ranks, self.order[0]))]
    reshape x1 -> x0, local copies, waits for them, and re-layouts: 1.29 us -> none  [on_device(): merge_gain.reshape(1, model_width)]
    ppermute x14 -> x13, waiting for transfers between devices: 27.9 us -> 26.7 us  [the longest x4 14.2 us: first(): lax.ppermute(sent, 'dp', flip_pairs(self.ranks, self.order[0]))]
    unnamed x32 -> x12, local copies, waits for them, and re-layouts: 1.26 us -> 0.02 us
  transfers between devices with their start and end apart: 20 -> 19, of which waited for: 9 -> 10; matrix products, arithmetic and copies ran while one was open for 3% -> 8% of each run, Pallas kernels for 20% -> 14%
where the time goes in v2:
time: 99.8 us; the launch traced here: 99.4 us
  Pallas kernels  33.6 us (34%)
  waiting for transfers between devices  33 us (33%)
  starting transfers between devices  23.1 us (23%)
  other arithmetic  7.48 us (7%)
  local copies, waits for them, and re-layouts  1.53 us (2%)
    pallas_call x1, Pallas kernels, run_forward(): pl.pallas_call(forward_kernel, out_shape=[jax.ShapeDtypeStruct(s, BF16) f...  19.4 us
    ppermute x4, waiting for transfers between devices, first(): lax.ppermute(sent, 'dp', flip_pairs(self.ranks, self.order[0]))  14.2 us
    ppermute x4, waiting for transfers between devices, step(): self.got = [lax.ppermute(sent, 'dp', flip_pairs(self.ranks, axis))]  11.4 us
    ppermute x6, starting transfers between devices, __init__(): self.got.append(lax.ppermute(row_of(k), 'vis', pairs))  10.4 us
    pallas_call x1, Pallas kernels, run_backward(): pl.pallas_call(backward_kernel, out_shape=[jax.ShapeDtypeStruct((h, pairs...  8 us
    ppermute x6, waiting for transfers between devices, __init__(): self.got.append(lax.ppermute(row_of(k), 'vis', pairs))  6.27 us
    pallas_call x3, Pallas kernels, product(): pl.pallas_call(functools.partial(product_kernel, pieces=taken, extra_at=e...  6.13 us
    ppermute x4, starting transfers between devices, first(): lax.ppermute(sent, 'dp', flip_pairs(self.ranks, self.order[0]))  5.95 us
  transfers between devices with their start and end apart: 19, of which 10 were waited for; matrix products, arithmetic and copies ran while one was open for 8% of the time, Pallas kernels for 14%

profile of v2, /device:TPU:0, one launch (start us, length us, event | category | flops | bytes accessed | tf_op | source)
XLA Modules:
  0.0 99.4 jit_solution(16681859057525370978)
XLA Ops:
  0.6 19.4 %shard_map.102 = (bf16[128,5120]{1,0:T(8,128)(2,1)}, bf16[4,3,960,128]{3,2,1,0:T(8,128)(2,1)}, bf16[4,12,128,128]{3,2,1,0:T(8,128)(2,1)}, bf16[4,960,128]{2,1,0:...) custom-call(s32[1]{0:T(128)} %bitcast.rank_ref, ...), custom_call_target="tpu_custom_call" | custom-call | flops 1 | bytes 1 | tf_op jit(solution)/shard_map/pallas_call | solution.py:418
  21.1 8.0 %shard_map.103 = (bf16[1024,512]{1,0:T(8,128)(2,1)}, bf16[1856,512]{1,0:T(8,128)(2,1)}) custom-call(bf16[4,3,960,128]{3,2,1,0:T(8,128)(2,1)} %get-tuple-element.48.packed_ref, bf16[4,12,128,128]{3,2,1,0:T(8,128)(2,1)} %get-tuple-element.49.probs_ref, bf16[4,960,128]{2,1,0:T(8,128)(2,1)} %get-tuple-element.50.d_context_ref), custom_call_target="tpu_custom_call" | custom-call | flops 1 | bytes 1 | tf_op jit(solution)/shard_map/pallas_call | solution.py:444
  29.3 1.7 %shard_map.104 = (bf16[2,160,1024]{2,1,0:T(8,128)(2,1)S(1)}, bf16[2,160,1024]{2,1,0:T(8,128)(2,1)S(1)}) custom-call(bf16[4,160,640]{2,1,0:T(8,128)(2,1)S(1)} %copy-done.4, bf16[4,160,640]{2,1,0:T(8,128)(2,1)S(1)} %collective-permute-done.1.other_ref, bf16[960,512]{1,0:T(8,128)(2,1)S(1)} %copy-done.3, bf16[960,512]{1,0:T(8,128)(2,1)S(1)} %collective-permute-done.right_other_ref), custom_call_target="tpu_custom_call" | custom-call | flops 1 | bytes 1 | tf_op jit(solution)/shard_map/pallas_call | solution.py:288
  32.2 2.8 %collective-permute-start.4 = (bf16[2,160,1024]{2,1,0:T(8,128)(2,1)S(1)}, bf16[2,160,1024]{2,1,0:T(8,128)(2,1)}, u32[]{:S(2)}, u32[]{:S(2)}) collective-permute-start(bf16[2,160,1024]{2,1,0:T(8,128)(2,1)S(1)} %get-tuple-element.60), channel_id=1, source_target_pairs={{0,8},{4,12},{8,0},{12,4},{16,24},{20,28},{24,16},{28,20},{1,9},{5... | collective-permute-start | bytes 1966088 | tf_op jit(solution)/shard_map/ppermute | solution.py:320
  35.1 1.5 %shard_map.105 = (bf16[2,160,1024]{2,1,0:T(8,128)(2,1)S(1)}, bf16[2,160,1024]{2,1,0:T(8,128)(2,1)S(1)}) custom-call(bf16[4,160,512]{2,1,0:T(8,128)(2,1)S(1)} %copy-done, bf16[4,160,512]{2,1,0:T(8,128)(2,1)S(1)} %collective-permute-done.2.other_ref, bf16[1024,512]{1,0:T(8,128)(2,1)S(1)} %copy-done.2, bf16[1024,512]{1,0:T(8,128)(2,1)S(1)} %collective-permute-done.3.right_other_ref), custom_call_target="tpu_custom_call" | custom-call | flops 1 | bytes 1 | tf_op jit(solution)/shard_map/pallas_call | solution.py:288
  36.6 1.6 %collective-permute-start.7 = (bf16[2,160,1024]{2,1,0:T(8,128)(2,1)S(1)}, bf16[2,160,1024]{2,1,0:T(8,128)(2,1)}, u32[]{:S(2)}, u32[]{:S(2)}) collective-permute-start(bf16[2,160,1024]{2,1,0:T(8,128)(2,1)S(1)} %get-tuple-element.71), channel_id=1, source_target_pairs={{0,16},{4,20},{8,24},{12,28},{16,0},{20,4},{24,8},{28,12},{1,17},{... | collective-permute-start | bytes 1966088 | tf_op jit(solution)/shard_map/ppermute | solution.py:320
  38.2 2.9 %shard_map.106 = (bf16[2,160,896]{2,1,0:T(8,128)(2,1)S(1)}, bf16[2,160,896]{2,1,0:T(8,128)(2,1)S(1)}, bf16[2,160,960]{2,1,0:T(8,128)(2,1)S(1)}, bf16[2,160,960]{2,1,0:T(8,128)(2,1)S(1)}) custom-call(bf16[4,160,512]{2,1,0:T(8,128)(2,1)S(1)} %copy-done, bf16[4,160,512]{2,1,0:T(8,128)(2,1)S(1)} %collective-permute-done.2.other_ref, ...), custom_call_target="tpu_custom_call" | custom-call | flops 1 | bytes 1 | tf_op jit(solution)/shard_map/pallas_call | solution.py:288
  41.1 9.1 %collective-permute-done.4 = bf16[2,160,1024]{2,1,0:T(8,128)(2,1)} collective-permute-done((bf16[2,160,1024]{2,1,0:T(8,128)(2,1)S(1)}, bf16[2,160,1024]{2,1,0:T(8,128)(2,1)}, u32[]{:S(2)}, u32[]{:S(2)}) %collective-permute-start.4) | collective-permute-done | bytes 655392 | tf_op jit(solution)/shard_map/ppermute | solution.py:320
  50.2 1.8 %fusion.5 = bf16[160,1024]{1,0:T(8,128)(2,1)} fusion(bf16[2,160,1024]{2,1,0:T(8,128)(2,1)} %collective-permute-done.4, bf16[2,160,1024]{2,1,0:T(8,128)(2,1)S(1)} %get-tuple-element.59), kind=kLoop, calls=%fused_computation.18 | loop fusion | flops 655360 | bytes 983040 | tf_op jit(solution)/shard_map/convert_element_type | solution.py:355
  52.1 1.8 %collective-permute-start.6 = (bf16[160,1024]{1,0:T(8,128)(2,1)}, bf16[160,1024]{1,0:T(8,128)(2,1)S(1)}, u32[]{:S(2)}, u32[]{:S(2)}) collective-permute-start(bf16[160,1024]{1,0:T(8,128)(2,1)} %fusion.5), channel_id=1, source_target_pairs={{0,16},{4,20},{8,24},{12,28},{16,0},{20,4},{24,8},{28,12},{1,17},{... | collective-permute-start | bytes 983048 | tf_op jit(solution)/shard_map/ppermute | solution.py:348
  53.8 1.8 %fusion.7 = bf16[160,1024]{1,0:T(8,128)(2,1)} fusion(bf16[2,160,1024]{2,1,0:T(8,128)(2,1)} %collective-permute-done.7, bf16[2,160,1024]{2,1,0:T(8,128)(2,1)S(1)} %get-tuple-element.70), kind=kLoop, calls=%fused_computation.20 | loop fusion | flops 655360 | bytes 983040 | tf_op jit(solution)/shard_map/convert_element_type | solution.py:355
  55.6 1.5 %collective-permute-start.8 = (bf16[160,1024]{1,0:T(8,128)(2,1)}, bf16[160,1024]{1,0:T(8,128)(2,1)}, u32[]{:S(2)}, u32[]{:S(2)}) collective-permute-start(bf16[160,1024]{1,0:T(8,128)(2,1)} %fusion.7), channel_id=1, source_target_pairs={{0,8},{4,12},{8,0},{12,4},{16,24},{20,28},{24,16},{28,20},{1,9},{5... | collective-permute-start | bytes 983048 | tf_op jit(solution)/shard_map/ppermute | solution.py:348
  58.6 4.2 %collective-permute-done.6 = bf16[160,1024]{1,0:T(8,128)(2,1)S(1)} collective-permute-done((bf16[160,1024]{1,0:T(8,128)(2,1)}, bf16[160,1024]{1,0:T(8,128)(2,1)S(1)}, u32[]{:S(2)}, u32[]{:S(2)}) %collective-permute-start.6) | collective-permute-done | bytes 327712 | tf_op jit(solution)/shard_map/ppermute | solution.py:348
  62.9 1.1 %fusion.2 = bf16[160,1024]{1,0:T(8,128)(2,1)S(1)} fusion(bf16[160,1024]{1,0:T(8,128)(2,1)S(1)} %collective-permute-done.6, bf16[2,160,1024]{2,1,0:T(8,128)(2,1)} %collective-permute-done.4, bf16[2,160,1024]{2,1,0:T(8,128)(2,1)S(1)} %get-tuple-element.59), kind=kLoop, calls=%fused_computation.5 | loop fusion | flops 1310720 | bytes 1310720 | tf_op jit(solution)/shard_map/convert_element_type | solution.py:365
  64.0 2.6 %collective-permute-done.8 = bf16[160,1024]{1,0:T(8,128)(2,1)} collective-permute-done((bf16[160,1024]{1,0:T(8,128)(2,1)}, bf16[160,1024]{1,0:T(8,128)(2,1)}, u32[]{:S(2)}, u32[]{:S(2)}) %collective-permute-start.8) | collective-permute-done | bytes 327712 | tf_op jit(solution)/shard_map/ppermute | solution.py:348
  66.6 1.2 %fusion.1 = bf16[160,1024]{1,0:T(8,128)(2,1)S(1)} fusion(bf16[160,1024]{1,0:T(8,128)(2,1)} %collective-permute-done.8, bf16[2,160,1024]{2,1,0:T(8,128)(2,1)} %collective-permute-done.7, bf16[2,160,1024]{2,1,0:T(8,128)(2,1)S(1)} %get-tuple-element.70), kind=kLoop, calls=%fused_computation.3 | loop fusion | flops 1310720 | bytes 1310720 | tf_op jit(solution)/shard_map/convert_element_type | solution.py:365
  67.9 3.6 %collective-permute-start.11 = (bf16[40,2048]{1,0:T(8,128)(2,1)S(1)}, bf16[40,2048]{1,0:T(8,128)(2,1)S(1)}, u32[]{:S(2)}, u32[]{:S(2)}) collective-permute-start(bf16[40,2048]{1,0:T(8,128)(2,1)S(1)} %pad_maximum_fusion.3), channel_id=1, source_target_pairs={{0,3},{1,0},{2,1},{3,2},{4,7},{5,4},{6,5},{7,6},{8,11},{9,8},{10,9... | collective-permute-start | bytes 491528 | tf_op jit(solution)/shard_map/ppermute | solution.py:388
  71.7 5.1 %collective-permute-done.12 = bf16[2,160,896]{2,1,0:T(8,128)(2,1)S(1)} collective-permute-done((bf16[2,160,896]{2,1,0:T(8,128)(2,1)}, bf16[2,160,896]{2,1,0:T(8,128)(2,1)S(1)}, u32[]{:S(2)}, u32[]{:S(2)}) %collective-permute-start.12) | collective-permute-done | bytes 573472 | tf_op jit(solution)/shard_map/ppermute | solution.py:320
  79.1 1.6 %collective-permute-start.9 = (bf16[40,2048]{1,0:T(8,128)(2,1)S(1)}, bf16[40,2048]{1,0:T(8,128)(2,1)S(1)}, u32[]{:S(2)}, u32[]{:S(2)}) collective-permute-start(bf16[40,2048]{1,0:T(8,128)(2,1)S(1)} %pad_maximum_fusion.1), channel_id=1, source_target_pairs={{0,1},{1,2},{2,3},{3,0},{4,5},{5,6},{6,7},{7,4},{8,9},{9,10},{10,1... | collective-permute-start | bytes 491528 | tf_op jit(solution)/shard_map/ppermute | solution.py:388
  80.7 3.0 %collective-permute-done.13 = bf16[160,896]{1,0:T(8,128)(2,1)S(1)} collective-permute-done((bf16[160,896]{1,0:T(8,128)(2,1)S(1)}, bf16[160,896]{1,0:T(8,128)(2,1)S(1)}, u32[]{:S(2)}, u32[]{:S(2)}) %collective-permute-start.13) | collective-permute-done | bytes 286752 | tf_op jit(solution)/shard_map/ppermute | solution.py:348
  83.9 1.5 %collective-permute-done.15 = bf16[160,960]{1,0:T(8,128)(2,1)S(1)} collective-permute-done((bf16[160,960]{1,0:T(8,128)(2,1)S(1)}, bf16[160,960]{1,0:T(8,128)(2,1)S(1)}, u32[]{:S(2)}, u32[]{:S(2)}) %collective-permute-start.15) | collective-permute-done | bytes 307232 | tf_op jit(solution)/shard_map/ppermute | solution.py:348
  87.4 2.6 %collective-permute-start.17 = (bf16[40,1856]{1,0:T(8,128)(2,1)S(1)}, bf16[40,1856]{1,0:T(8,128)(2,1)S(1)}, u32[]{:S(2)}, u32[]{:S(2)}) collective-permute-start(bf16[40,1856]{1,0:T(8,128)(2,1)S(1)} %pad_maximum_fusion.5), channel_id=1, source_target_pairs={{0,2},{1,3},{2,0},{3,1},{4,6},{5,7},{6,4},{7,5},{8,10},{9,11},{10,... | collective-permute-start | bytes 445448 | tf_op jit(solution)/shard_map/ppermute | solution.py:388
  90.0 1.4 %collective-permute-start.18 = (bf16[40,1856]{1,0:T(8,128)(2,1)S(1)}, bf16[40,1856]{1,0:T(8,128)(2,1)S(1)}, u32[]{:S(2)}, u32[]{:S(2)}) collective-permute-start(bf16[40,1856]{1,0:T(8,128)(2,1)S(1)} %pad_maximum_fusion.6), channel_id=1, source_target_pairs={{0,3},{1,0},{2,1},{3,2},{4,7},{5,4},{6,5},{7,6},{8,11},{9,8},{10,9... | collective-permute-start | bytes 445448 | tf_op jit(solution)/shard_map/ppermute | solution.py:388
  94.0 4.5 %collective-permute-done.17 = bf16[40,1856]{1,0:T(8,128)(2,1)S(1)} collective-permute-done((bf16[40,1856]{1,0:T(8,128)(2,1)S(1)}, bf16[40,1856]{1,0:T(8,128)(2,1)S(1)}, u32[]{:S(2)}, u32[]{:S(2)}) %collective-permute-start.17) | collective-permute-done | bytes 148512 | tf_op jit(solution)/shard_map/ppermute | solution.py:388
  (54 shorter events, 11.9 us)
Async XLA Ops:
  20.1 9.1 %collective-permute-start = (bf16[960,512]{1,0:T(8,128)(2,1)}, bf16[960,512]{1,0:T(8,128)(2,1)S(1)}, u32[]{:S(2)}, u32[]{:S(2)}) collective-permute-start(bf16[960,512]{1,0:T(8,128)(2,1)} %get-tuple-element.45.right_ref), channel_id=1, source_target_pairs={{0,4},{4,0},{8,12},{12,8},{16,20},{20,16},{24,28},{28,24},{1,5},{5... | collective-permute-start | bytes 2949128 | tf_op jit(solution)/shard_map/ppermute | solution.py:473
  20.6 8.5 %collective-permute-start.1 = (bf16[4,160,640]{2,1,0:T(8,128)(2,1)}, bf16[4,160,640]{2,1,0:T(8,128)(2,1)S(1)}, u32[]{:S(2)}, u32[]{:S(2)}) collective-permute-start(bf16[4,160,640]{2,1,0:T(8,128)(2,1)} %get-tuple-element.46), channel_id=1, source_target_pairs={{0,4},{4,0},{8,12},{12,8},{16,20},{20,16},{24,28},{28,24},{1,5},{5... | collective-permute-start | bytes 2457608 | tf_op jit(solution)/shard_map/ppermute | solution.py:473
  20.7 8.4 %collective-permute-start.2 = (bf16[4,160,512]{2,1,0:T(8,128)(2,1)}, bf16[4,160,512]{2,1,0:T(8,128)(2,1)S(1)}, u32[]{:S(2)}, u32[]{:S(2)}) collective-permute-start(bf16[4,160,512]{2,1,0:T(8,128)(2,1)} %get-tuple-element.47), channel_id=1, source_target_pairs={{0,4},{4,0},{8,12},{12,8},{16,20},{20,16},{24,28},{28,24},{1,5},{5... | collective-permute-start | bytes 1966088 | tf_op jit(solution)/shard_map/ppermute | solution.py:473
  21.1 8.2 %copy-start.3 = (bf16[960,512]{1,0:T(8,128)(2,1)S(1)}, bf16[960,512]{1,0:T(8,128)(2,1)}, u32[]{:S(2)}) copy-start(bf16[960,512]{1,0:T(8,128)(2,1)} %get-tuple-element.45.right_ref) | copy-start | bytes 2949124
  21.1 8.2 %copy-start.4 = (bf16[4,160,640]{2,1,0:T(8,128)(2,1)S(1)}, bf16[4,160,640]{2,1,0:T(8,128)(2,1)}, u32[]{:S(2)}) copy-start(bf16[4,160,640]{2,1,0:T(8,128)(2,1)} %get-tuple-element.55.keep_ref) | copy-start | bytes 2457604
  29.1 6.0 %copy-start = (bf16[4,160,512]{2,1,0:T(8,128)(2,1)S(1)}, bf16[4,160,512]{2,1,0:T(8,128)(2,1)}, u32[]{:S(2)}) copy-start(bf16[4,160,512]{2,1,0:T(8,128)(2,1)} %get-tuple-element.61.keep_ref) | copy-start | bytes 1966084
  29.1 6.0 %copy-start.2 = (bf16[1024,512]{1,0:T(8,128)(2,1)S(1)}, bf16[1024,512]{1,0:T(8,128)(2,1)}, u32[]{:S(2)}) copy-start(bf16[1024,512]{1,0:T(8,128)(2,1)} %get-tuple-element.53.right_ref) | copy-start | bytes 3145732
  29.2 2.9 %collective-permute-start.3 = (bf16[1024,512]{1,0:T(8,128)(2,1)}, bf16[1024,512]{1,0:T(8,128)(2,1)S(1)}, u32[]{:S(2)}, u32[]{:S(2)}) collective-permute-start(bf16[1024,512]{1,0:T(8,128)(2,1)} %get-tuple-element.53.right_ref), channel_id=1, source_target_pairs={{0,4},{4,0},{8,12},{12,8},{16,20},{20,16},{24,28},{28,24},{1,5},{5... | collective-permute-start | bytes 3145736 | tf_op jit(solution)/shard_map/ppermute | solution.py:473
  32.1 6.1 %collective-permute-start.5 = (bf16[1856,512]{1,0:T(8,128)(2,1)S(1)}, bf16[1856,512]{1,0:T(8,128)(2,1)S(1)}, u32[]{:S(2)}, u32[]{:S(2)}) collective-permute-start(bf16[1856,512]{1,0:T(8,128)(2,1)S(1)} %copy-done.1), channel_id=1, source_target_pairs={{0,4},{4,0},{8,12},{12,8},{16,20},{20,16},{24,28},{28,24},{1,5},{5... | collective-permute-start | bytes 5701640 | tf_op jit(solution)/shard_map/ppermute | solution.py:473
  32.2 18.0 %collective-permute-start.4 = (bf16[2,160,1024]{2,1,0:T(8,128)(2,1)S(1)}, bf16[2,160,1024]{2,1,0:T(8,128)(2,1)}, u32[]{:S(2)}, u32[]{:S(2)}) collective-permute-start(bf16[2,160,1024]{2,1,0:T(8,128)(2,1)S(1)} %get-tuple-element.60), channel_id=1, source_target_pairs={{0,8},{4,12},{8,0},{12,4},{16,24},{20,28},{24,16},{28,20},{1,9},{5... | collective-permute-start | bytes 1966088 | tf_op jit(solution)/shard_map/ppermute | solution.py:320
  36.6 17.2 %collective-permute-start.7 = (bf16[2,160,1024]{2,1,0:T(8,128)(2,1)S(1)}, bf16[2,160,1024]{2,1,0:T(8,128)(2,1)}, u32[]{:S(2)}, u32[]{:S(2)}) collective-permute-start(bf16[2,160,1024]{2,1,0:T(8,128)(2,1)S(1)} %get-tuple-element.71), channel_id=1, source_target_pairs={{0,16},{4,20},{8,24},{12,28},{16,0},{20,4},{24,8},{28,12},{1,17},{... | collective-permute-start | bytes 1966088 | tf_op jit(solution)/shard_map/ppermute | solution.py:320
  41.1 12.7 %copy-start.5 = (bf16[2,160,896]{2,1,0:T(8,128)(2,1)}, bf16[2,160,896]{2,1,0:T(8,128)(2,1)S(1)}, u32[]{:S(2)}) copy-start(bf16[2,160,896]{2,1,0:T(8,128)(2,1)S(1)} %get-tuple-element.76) | copy-start | bytes 1720324
  52.1 10.8 %collective-permute-start.6 = (bf16[160,1024]{1,0:T(8,128)(2,1)}, bf16[160,1024]{1,0:T(8,128)(2,1)S(1)}, u32[]{:S(2)}, u32[]{:S(2)}) collective-permute-start(bf16[160,1024]{1,0:T(8,128)(2,1)} %fusion.5), channel_id=1, source_target_pairs={{0,16},{4,20},{8,24},{12,28},{16,0},{20,4},{24,8},{28,12},{1,17},{... | collective-permute-start | bytes 983048 | tf_op jit(solution)/shard_map/ppermute | solution.py:348
  55.6 11.0 %collective-permute-start.8 = (bf16[160,1024]{1,0:T(8,128)(2,1)}, bf16[160,1024]{1,0:T(8,128)(2,1)}, u32[]{:S(2)}, u32[]{:S(2)}) collective-permute-start(bf16[160,1024]{1,0:T(8,128)(2,1)} %fusion.7), channel_id=1, source_target_pairs={{0,8},{4,12},{8,0},{12,4},{16,24},{20,28},{24,16},{28,20},{1,9},{5... | collective-permute-start | bytes 983048 | tf_op jit(solution)/shard_map/ppermute | solution.py:348
  57.1 20.7 %collective-permute-start.14 = (bf16[2,160,960]{2,1,0:T(8,128)(2,1)S(1)}, bf16[2,160,960]{2,1,0:T(8,128)(2,1)S(1)}, u32[]{:S(2)}, u32[]{:S(2)}) collective-permute-start(bf16[2,160,960]{2,1,0:T(8,128)(2,1)S(1)} %get-tuple-element.78), channel_id=1, source_target_pairs={{0,16},{4,20},{8,24},{12,28},{16,0},{20,4},{24,8},{28,12},{1,17},{... | collective-permute-start | bytes 1843208 | tf_op jit(solution)/shard_map/ppermute | solution.py:320
  57.6 19.1 %collective-permute-start.12 = (bf16[2,160,896]{2,1,0:T(8,128)(2,1)}, bf16[2,160,896]{2,1,0:T(8,128)(2,1)S(1)}, u32[]{:S(2)}, u32[]{:S(2)}) collective-permute-start(bf16[2,160,896]{2,1,0:T(8,128)(2,1)} %copy-done.5), channel_id=1, source_target_pairs={{0,8},{4,12},{8,0},{12,4},{16,24},{20,28},{24,16},{28,20},{1,9},{5... | collective-permute-start | bytes 1720328 | tf_op jit(solution)/shard_map/ppermute | solution.py:320
  67.9 17.7 %collective-permute-start.11 = (bf16[40,2048]{1,0:T(8,128)(2,1)S(1)}, bf16[40,2048]{1,0:T(8,128)(2,1)S(1)}, u32[]{:S(2)}, u32[]{:S(2)}) collective-permute-start(bf16[40,2048]{1,0:T(8,128)(2,1)S(1)} %pad_maximum_fusion.3), channel_id=1, source_target_pairs={{0,3},{1,0},{2,1},{3,2},{4,7},{5,4},{6,5},{7,6},{8,11},{9,8},{10,9... | collective-permute-start | bytes 491528 | tf_op jit(solution)/shard_map/ppermute | solution.py:388
  71.6 14.0 %collective-permute-start.10 = (bf16[40,2048]{1,0:T(8,128)(2,1)S(1)}, bf16[40,2048]{1,0:T(8,128)(2,1)S(1)}, u32[]{:S(2)}, u32[]{:S(2)}) collective-permute-start(bf16[40,2048]{1,0:T(8,128)(2,1)S(1)} %pad_maximum_fusion.2), channel_id=1, source_target_pairs={{0,2},{1,3},{2,0},{3,1},{4,6},{5,7},{6,4},{7,5},{8,10},{9,11},{10,... | collective-permute-start | bytes 491528 | tf_op jit(solution)/shard_map/ppermute | solution.py:388
  76.8 6.9 %collective-permute-start.13 = (bf16[160,896]{1,0:T(8,128)(2,1)S(1)}, bf16[160,896]{1,0:T(8,128)(2,1)S(1)}, u32[]{:S(2)}, u32[]{:S(2)}) collective-permute-start(bf16[160,896]{1,0:T(8,128)(2,1)S(1)} %fusion.11), channel_id=1, source_target_pairs={{0,16},{4,20},{8,24},{12,28},{16,0},{20,4},{24,8},{28,12},{1,17},{... | collective-permute-start | bytes 860168 | tf_op jit(solution)/shard_map/ppermute | solution.py:348
  78.0 7.5 %collective-permute-start.15 = (bf16[160,960]{1,0:T(8,128)(2,1)S(1)}, bf16[160,960]{1,0:T(8,128)(2,1)S(1)}, u32[]{:S(2)}, u32[]{:S(2)}) collective-permute-start(bf16[160,960]{1,0:T(8,128)(2,1)S(1)} %fusion.9), channel_id=1, source_target_pairs={{0,8},{4,12},{8,0},{12,4},{16,24},{20,28},{24,16},{28,20},{1,9},{5... | collective-permute-start | bytes 921608 | tf_op jit(solution)/shard_map/ppermute | solution.py:348
  79.1 7.2 %collective-permute-start.9 = (bf16[40,2048]{1,0:T(8,128)(2,1)S(1)}, bf16[40,2048]{1,0:T(8,128)(2,1)S(1)}, u32[]{:S(2)}, u32[]{:S(2)}) collective-permute-start(bf16[40,2048]{1,0:T(8,128)(2,1)S(1)} %pad_maximum_fusion.1), channel_id=1, source_target_pairs={{0,1},{1,2},{2,3},{3,0},{4,5},{5,6},{6,7},{7,4},{8,9},{9,10},{10,1... | collective-permute-start | bytes 491528 | tf_op jit(solution)/shard_map/ppermute | solution.py:388
  86.4 7.7 %collective-permute-start.16 = (bf16[40,1856]{1,0:T(8,128)(2,1)S(1)}, bf16[40,1856]{1,0:T(8,128)(2,1)S(1)}, u32[]{:S(2)}, u32[]{:S(2)}) collective-permute-start(bf16[40,1856]{1,0:T(8,128)(2,1)S(1)} %pad_maximum_fusion.4), channel_id=1, source_target_pairs={{0,1},{1,2},{2,3},{3,0},{4,5},{5,6},{6,7},{7,4},{8,9},{9,10},{10,1... | collective-permute-start | bytes 445448 | tf_op jit(solution)/shard_map/ppermute | solution.py:388
  87.4 11.1 %collective-permute-start.17 = (bf16[40,1856]{1,0:T(8,128)(2,1)S(1)}, bf16[40,1856]{1,0:T(8,128)(2,1)S(1)}, u32[]{:S(2)}, u32[]{:S(2)}) collective-permute-start(bf16[40,1856]{1,0:T(8,128)(2,1)S(1)} %pad_maximum_fusion.5), channel_id=1, source_target_pairs={{0,2},{1,3},{2,0},{3,1},{4,6},{5,7},{6,4},{7,5},{8,10},{9,11},{10,... | collective-permute-start | bytes 445448 | tf_op jit(solution)/shard_map/ppermute | solution.py:388
  90.0 8.5 %collective-permute-start.18 = (bf16[40,1856]{1,0:T(8,128)(2,1)S(1)}, bf16[40,1856]{1,0:T(8,128)(2,1)S(1)}, u32[]{:S(2)}, u32[]{:S(2)}) collective-permute-start(bf16[40,1856]{1,0:T(8,128)(2,1)S(1)} %pad_maximum_fusion.6), channel_id=1, source_target_pairs={{0,3},{1,0},{2,1},{3,2},{4,7},{5,4},{6,5},{7,6},{8,11},{9,8},{10,9... | collective-permute-start | bytes 445448 | tf_op jit(solution)/shard_map/ppermute | solution.py:388
  (1 other events, 3.0 us)

commit v3 on v2

--- a/solution.py
+++ b/solution.py
@@ -8,7 +8,7 @@
 from jax.sharding import PartitionSpec as P
 
 HEADS = 12
-STAGE = 4
+STAGE = 12
 JOIN = 4
 PAIR = 2
 LANES = 128
@@ -102,12 +102,16 @@
     for at, size in tiles(model_width):
         rows_ref[:, at:at + size] = dot(chosen_ref[...], patches_ref[:, at:at + size])
 
+    @pl.loop(0, row_count // strip)
+    def _(n):
+        here = pl.ds(pl.multiple_of(n * strip, strip), strip)
+        rows = rows_ref[here, :]
+        power = jnp.mean(rows * rows, axis=1, keepdims=True)
+        d_att_ref[here, :] = (rows * lax.rsqrt(power + EPSILON)).astype(BF16)
+
     for pair in range(pairs):
         here = slice(pair * block, (pair + 1) * block)
-        rows = rows_ref[here, :]
-        power = jnp.mean(rows * rows, axis=1, keepdims=True)
-        normed = (rows * lax.rsqrt(power + EPSILON)).astype(BF16)
-        norm_ref[:, here] = normed.T
+        norm_ref[:, here] = d_att_ref[here, :].T
     by_core(norm_ref, norm_keep_ref, norm_send_ref)
     give(0, norm_keep_ref, norm_keep_hbm)
     give(1, norm_send_ref, norm_send_hbm)
@@ -161,15 +165,16 @@
     gain_sum_ref[...] = jnp.zeros_like(gain_sum_ref)
     load_cot.wait()
 
-    @pl.loop(0, pairs)
-    def _(pair):
-        row_at = lax.broadcasted_iota(jnp.int32, (strip, 1), 0)
-        alive = alive_of(row_at, live_ref[0, PAIR * pair], live_ref[0, PAIR * pair + 1], group)
-        alive = jnp.where(alive, 1.0, 0.0)
+    @pl.loop(0, pairs * PAIR)
+    def _(window):
+        pair, second = window // PAIR, window % PAIR
+        row_at = lax.broadcasted_iota(jnp.int32, (group, 1), 0)
+        alive = jnp.where(row_at * JOIN < live_ref[0, window], 1.0, 0.0)
         gain = gain_ref[...].reshape(1, model_width)
-        out_rows = pl.ds(pl.multiple_of(pair * strip, strip), strip)
+        out_rows = pl.ds(pl.multiple_of(window * group, group), group)
         for turn in range(JOIN):
-            here = pl.ds(pl.multiple_of(pair * block + turn * strip, strip), strip)
+            start = pair * block + turn * strip + second * group
+            here = pl.ds(pl.multiple_of(start, group), group)
             columns = slice(turn * model_width, (turn + 1) * model_width)
             attended = rows_ref[here, :]
             power = jnp.mean(attended * attended, axis=1, keepdims=True)
@@ -178,7 +183,7 @@
             merged_ref[out_rows, columns] = (normalized * gain * alive).astype(BF16)
             grad_rows = cot_ref[out_rows, columns].astype(F32) * alive
             crossed = grad_rows * normalized
-            gain_sum_ref[...] += jnp.sum(crossed.reshape(strip // 8, 8, model_width), axis=0)
+            gain_sum_ref[...] += jnp.sum(crossed.reshape(group // 8, 8, model_width), axis=0)
             mean = jnp.mean(crossed * gain, axis=1, keepdims=True)
             d_att_ref[here, :] = (inverse * (grad_rows * gain - normalized * mean)).astype(BF16)
 
@@ -290,7 +295,7 @@
         out_shape=shapes,
         in_specs=[VMEM] * 4,
         out_specs=[VMEM] * len(shapes),
-        compiler_params=pltpu.CompilerParams(vmem_limit_bytes=24 * 2**20),
+        compiler_params=pltpu.CompilerParams(vmem_limit_bytes=14 * 2**20),
         cost_estimate=SMALL,
     )(keep, other, *right)
     return [found[sum(counts[:n]):sum(counts[:n + 1])] for n in range(len(counts))]

time: 99.8 us -> 99.9 us (level)
  transfers between devices with their start and end apart: 19 -> 19, of which waited for: 10 -> 10; matrix products, arithmetic and copies ran while one was open for 8% -> 8% of each run, Pallas kernels for 14% -> 13%
where the time goes in v3:
time: 99.9 us; the launch traced here: 99.5 us
  Pallas kernels  33.6 us (34%)
  waiting for transfers between devices  33 us (33%)
  starting transfers between devices  23.1 us (23%)
  other arithmetic  7.48 us (7%)
  local copies, waits for them, and re-layouts  1.53 us (2%)
    pallas_call x1, Pallas kernels, run_forward(): pl.pallas_call(forward_kernel, out_shape=[jax.ShapeDtypeStruct(s, BF16) f...  20.3 us
    ppermute x4, waiting for transfers between devices, first(): lax.ppermute(sent, 'dp', flip_pairs(self.ranks, self.order[0]))  14.2 us
    ppermute x4, waiting for transfers between devices, step(): self.got = [lax.ppermute(sent, 'dp', flip_pairs(self.ranks, axis))]  11.4 us
    ppermute x6, starting transfers between devices, __init__(): self.got.append(lax.ppermute(row_of(k), 'vis', pairs))  10.4 us
    pallas_call x1, Pallas kernels, run_backward(): pl.pallas_call(backward_kernel, out_shape=[jax.ShapeDtypeStruct((h, pairs...  7.18 us
    ppermute x6, waiting for transfers between devices, __init__(): self.got.append(lax.ppermute(row_of(k), 'vis', pairs))  6.31 us
    pallas_call x3, Pallas kernels, product(): pl.pallas_call(functools.partial(product_kernel, pieces=taken, extra_at=e...  6.1 us
    ppermute x4, starting transfers between devices, first(): lax.ppermute(sent, 'dp', flip_pairs(self.ranks, self.order[0]))  5.97 us
  transfers between devices with their start and end apart: 19, of which 10 were waited for; matrix products, arithmetic and copies ran while one was open for 8% of the time, Pallas kernels for 13%

profile of v3, /device:TPU:0, one launch (start us, length us, event | category | flops | bytes accessed | tf_op | source)
XLA Modules:
  0.0 99.5 jit_solution(2838103316546888290)
XLA Ops:
  0.6 20.3 %shard_map.102 = (bf16[128,5120]{1,0:T(8,128)(2,1)}, bf16[4,3,960,128]{3,2,1,0:T(8,128)(2,1)}, bf16[4,12,128,128]{3,2,1,0:T(8,128)(2,1)}, bf16[4,960,128]{2,1,0:...) custom-call(s32[1]{0:T(128)} %bitcast.rank_ref, ...), custom_call_target="tpu_custom_call" | custom-call | flops 1 | bytes 1 | tf_op jit(solution)/shard_map/pallas_call | solution.py:423
  22.0 7.2 %shard_map.103 = (bf16[1024,512]{1,0:T(8,128)(2,1)}, bf16[1856,512]{1,0:T(8,128)(2,1)}) custom-call(bf16[4,3,960,128]{3,2,1,0:T(8,128)(2,1)} %get-tuple-element.48.packed_ref, bf16[4,12,128,128]{3,2,1,0:T(8,128)(2,1)} %get-tuple-element.49.probs_ref, bf16[4,960,128]{2,1,0:T(8,128)(2,1)} %get-tuple-element.50.d_context_ref), custom_call_target="tpu_custom_call" | custom-call | flops 1 | bytes 1 | tf_op jit(solution)/shard_map/pallas_call | solution.py:449
  29.4 1.6 %shard_map.104 = (bf16[2,160,1024]{2,1,0:T(8,128)(2,1)S(1)}, bf16[2,160,1024]{2,1,0:T(8,128)(2,1)S(1)}) custom-call(bf16[4,160,640]{2,1,0:T(8,128)(2,1)S(1)} %copy-done.4, bf16[4,160,640]{2,1,0:T(8,128)(2,1)S(1)} %collective-permute-done.1.other_ref, bf16[960,512]{1,0:T(8,128)(2,1)S(1)} %copy-done.3, bf16[960,512]{1,0:T(8,128)(2,1)S(1)} %collective-permute-done.right_other_ref), custom_call_target="tpu_custom_call" | custom-call | flops 1 | bytes 1 | tf_op jit(solution)/shard_map/pallas_call | solution.py:293
  32.3 2.9 %collective-permute-start.4 = (bf16[2,160,1024]{2,1,0:T(8,128)(2,1)S(1)}, bf16[2,160,1024]{2,1,0:T(8,128)(2,1)}, u32[]{:S(2)}, u32[]{:S(2)}) collective-permute-start(bf16[2,160,1024]{2,1,0:T(8,128)(2,1)S(1)} %get-tuple-element.60), channel_id=1, source_target_pairs={{0,8},{4,12},{8,0},{12,4},{16,24},{20,28},{24,16},{28,20},{1,9},{5... | collective-permute-start | bytes 1966088 | tf_op jit(solution)/shard_map/ppermute | solution.py:325
  35.2 1.5 %shard_map.105 = (bf16[2,160,1024]{2,1,0:T(8,128)(2,1)S(1)}, bf16[2,160,1024]{2,1,0:T(8,128)(2,1)S(1)}) custom-call(bf16[4,160,512]{2,1,0:T(8,128)(2,1)S(1)} %copy-done, bf16[4,160,512]{2,1,0:T(8,128)(2,1)S(1)} %collective-permute-done.2.other_ref, bf16[1024,512]{1,0:T(8,128)(2,1)S(1)} %copy-done.2, bf16[1024,512]{1,0:T(8,128)(2,1)S(1)} %collective-permute-done.3.right_other_ref), custom_call_target="tpu_custom_call" | custom-call | flops 1 | bytes 1 | tf_op jit(solution)/shard_map/pallas_call | solution.py:293
  36.8 1.6 %collective-permute-start.7 = (bf16[2,160,1024]{2,1,0:T(8,128)(2,1)S(1)}, bf16[2,160,1024]{2,1,0:T(8,128)(2,1)}, u32[]{:S(2)}, u32[]{:S(2)}) collective-permute-start(bf16[2,160,1024]{2,1,0:T(8,128)(2,1)S(1)} %get-tuple-element.71), channel_id=1, source_target_pairs={{0,16},{4,20},{8,24},{12,28},{16,0},{20,4},{24,8},{28,12},{1,17},{... | collective-permute-start | bytes 1966088 | tf_op jit(solution)/shard_map/ppermute | solution.py:325
  38.3 2.9 %shard_map.106 = (bf16[2,160,896]{2,1,0:T(8,128)(2,1)S(1)}, bf16[2,160,896]{2,1,0:T(8,128)(2,1)S(1)}, bf16[2,160,960]{2,1,0:T(8,128)(2,1)S(1)}, bf16[2,160,960]{2,1,0:T(8,128)(2,1)S(1)}) custom-call(bf16[4,160,512]{2,1,0:T(8,128)(2,1)S(1)} %copy-done, bf16[4,160,512]{2,1,0:T(8,128)(2,1)S(1)} %collective-permute-done.2.other_ref, ...), custom_call_target="tpu_custom_call" | custom-call | flops 1 | bytes 1 | tf_op jit(solution)/shard_map/pallas_call | solution.py:293
  41.2 9.1 %collective-permute-done.4 = bf16[2,160,1024]{2,1,0:T(8,128)(2,1)} collective-permute-done((bf16[2,160,1024]{2,1,0:T(8,128)(2,1)S(1)}, bf16[2,160,1024]{2,1,0:T(8,128)(2,1)}, u32[]{:S(2)}, u32[]{:S(2)}) %collective-permute-start.4) | collective-permute-done | bytes 655392 | tf_op jit(solution)/shard_map/ppermute | solution.py:325
  50.3 1.8 %fusion.5 = bf16[160,1024]{1,0:T(8,128)(2,1)} fusion(bf16[2,160,1024]{2,1,0:T(8,128)(2,1)} %collective-permute-done.4, bf16[2,160,1024]{2,1,0:T(8,128)(2,1)S(1)} %get-tuple-element.59), kind=kLoop, calls=%fused_computation.18 | loop fusion | flops 655360 | bytes 983040 | tf_op jit(solution)/shard_map/convert_element_type | solution.py:360
  52.2 1.7 %collective-permute-start.6 = (bf16[160,1024]{1,0:T(8,128)(2,1)}, bf16[160,1024]{1,0:T(8,128)(2,1)S(1)}, u32[]{:S(2)}, u32[]{:S(2)}) collective-permute-start(bf16[160,1024]{1,0:T(8,128)(2,1)} %fusion.5), channel_id=1, source_target_pairs={{0,16},{4,20},{8,24},{12,28},{16,0},{20,4},{24,8},{28,12},{1,17},{... | collective-permute-start | bytes 983048 | tf_op jit(solution)/shard_map/ppermute | solution.py:353
  53.9 1.8 %fusion.7 = bf16[160,1024]{1,0:T(8,128)(2,1)} fusion(bf16[2,160,1024]{2,1,0:T(8,128)(2,1)} %collective-permute-done.7, bf16[2,160,1024]{2,1,0:T(8,128)(2,1)S(1)} %get-tuple-element.70), kind=kLoop, calls=%fused_computation.20 | loop fusion | flops 655360 | bytes 983040 | tf_op jit(solution)/shard_map/convert_element_type | solution.py:360
  55.7 1.5 %collective-permute-start.8 = (bf16[160,1024]{1,0:T(8,128)(2,1)}, bf16[160,1024]{1,0:T(8,128)(2,1)}, u32[]{:S(2)}, u32[]{:S(2)}) collective-permute-start(bf16[160,1024]{1,0:T(8,128)(2,1)} %fusion.7), channel_id=1, source_target_pairs={{0,8},{4,12},{8,0},{12,4},{16,24},{20,28},{24,16},{28,20},{1,9},{5... | collective-permute-start | bytes 983048 | tf_op jit(solution)/shard_map/ppermute | solution.py:353
  58.7 4.3 %collective-permute-done.6 = bf16[160,1024]{1,0:T(8,128)(2,1)S(1)} collective-permute-done((bf16[160,1024]{1,0:T(8,128)(2,1)}, bf16[160,1024]{1,0:T(8,128)(2,1)S(1)}, u32[]{:S(2)}, u32[]{:S(2)}) %collective-permute-start.6) | collective-permute-done | bytes 327712 | tf_op jit(solution)/shard_map/ppermute | solution.py:353
  64.1 2.5 %collective-permute-done.8 = bf16[160,1024]{1,0:T(8,128)(2,1)} collective-permute-done((bf16[160,1024]{1,0:T(8,128)(2,1)}, bf16[160,1024]{1,0:T(8,128)(2,1)}, u32[]{:S(2)}, u32[]{:S(2)}) %collective-permute-start.8) | collective-permute-done | bytes 327712 | tf_op jit(solution)/shard_map/ppermute | solution.py:353
  66.7 1.2 %fusion.1 = bf16[160,1024]{1,0:T(8,128)(2,1)S(1)} fusion(bf16[160,1024]{1,0:T(8,128)(2,1)} %collective-permute-done.8, bf16[2,160,1024]{2,1,0:T(8,128)(2,1)} %collective-permute-done.7, bf16[2,160,1024]{2,1,0:T(8,128)(2,1)S(1)} %get-tuple-element.70), kind=kLoop, calls=%fused_computation.3 | loop fusion | flops 1310720 | bytes 1310720 | tf_op jit(solution)/shard_map/convert_element_type | solution.py:370
  68.0 3.7 %collective-permute-start.11 = (bf16[40,2048]{1,0:T(8,128)(2,1)S(1)}, bf16[40,2048]{1,0:T(8,128)(2,1)S(1)}, u32[]{:S(2)}, u32[]{:S(2)}) collective-permute-start(bf16[40,2048]{1,0:T(8,128)(2,1)S(1)} %pad_maximum_fusion.3), channel_id=1, source_target_pairs={{0,3},{1,0},{2,1},{3,2},{4,7},{5,4},{6,5},{7,6},{8,11},{9,8},{10,9... | collective-permute-start | bytes 491528 | tf_op jit(solution)/shard_map/ppermute | solution.py:393
  71.8 5.1 %collective-permute-done.12 = bf16[2,160,896]{2,1,0:T(8,128)(2,1)S(1)} collective-permute-done((bf16[2,160,896]{2,1,0:T(8,128)(2,1)}, bf16[2,160,896]{2,1,0:T(8,128)(2,1)S(1)}, u32[]{:S(2)}, u32[]{:S(2)}) %collective-permute-start.12) | collective-permute-done | bytes 573472 | tf_op jit(solution)/shard_map/ppermute | solution.py:325
  78.1 1.1 %collective-permute-start.15 = (bf16[160,960]{1,0:T(8,128)(2,1)S(1)}, bf16[160,960]{1,0:T(8,128)(2,1)S(1)}, u32[]{:S(2)}, u32[]{:S(2)}) collective-permute-start(bf16[160,960]{1,0:T(8,128)(2,1)S(1)} %fusion.9), channel_id=1, source_target_pairs={{0,8},{4,12},{8,0},{12,4},{16,24},{20,28},{24,16},{28,20},{1,9},{5... | collective-permute-start | bytes 921608 | tf_op jit(solution)/shard_map/ppermute | solution.py:353
  79.2 1.6 %collective-permute-start.9 = (bf16[40,2048]{1,0:T(8,128)(2,1)S(1)}, bf16[40,2048]{1,0:T(8,128)(2,1)S(1)}, u32[]{:S(2)}, u32[]{:S(2)}) collective-permute-start(bf16[40,2048]{1,0:T(8,128)(2,1)S(1)} %pad_maximum_fusion.1), channel_id=1, source_target_pairs={{0,1},{1,2},{2,3},{3,0},{4,5},{5,6},{6,7},{7,4},{8,9},{9,10},{10,1... | collective-permute-start | bytes 491528 | tf_op jit(solution)/shard_map/ppermute | solution.py:393
  80.8 3.0 %collective-permute-done.13 = bf16[160,896]{1,0:T(8,128)(2,1)S(1)} collective-permute-done((bf16[160,896]{1,0:T(8,128)(2,1)S(1)}, bf16[160,896]{1,0:T(8,128)(2,1)S(1)}, u32[]{:S(2)}, u32[]{:S(2)}) %collective-permute-start.13) | collective-permute-done | bytes 286752 | tf_op jit(solution)/shard_map/ppermute | solution.py:353
  83.9 1.6 %collective-permute-done.15 = bf16[160,960]{1,0:T(8,128)(2,1)S(1)} collective-permute-done((bf16[160,960]{1,0:T(8,128)(2,1)S(1)}, bf16[160,960]{1,0:T(8,128)(2,1)S(1)}, u32[]{:S(2)}, u32[]{:S(2)}) %collective-permute-start.15) | collective-permute-done | bytes 307232 | tf_op jit(solution)/shard_map/ppermute | solution.py:353
  87.5 2.6 %collective-permute-start.17 = (bf16[40,1856]{1,0:T(8,128)(2,1)S(1)}, bf16[40,1856]{1,0:T(8,128)(2,1)S(1)}, u32[]{:S(2)}, u32[]{:S(2)}) collective-permute-start(bf16[40,1856]{1,0:T(8,128)(2,1)S(1)} %pad_maximum_fusion.5), channel_id=1, source_target_pairs={{0,2},{1,3},{2,0},{3,1},{4,6},{5,7},{6,4},{7,5},{8,10},{9,11},{10,... | collective-permute-start | bytes 445448 | tf_op jit(solution)/shard_map/ppermute | solution.py:393
  90.1 1.4 %collective-permute-start.18 = (bf16[40,1856]{1,0:T(8,128)(2,1)S(1)}, bf16[40,1856]{1,0:T(8,128)(2,1)S(1)}, u32[]{:S(2)}, u32[]{:S(2)}) collective-permute-start(bf16[40,1856]{1,0:T(8,128)(2,1)S(1)} %pad_maximum_fusion.6), channel_id=1, source_target_pairs={{0,3},{1,0},{2,1},{3,2},{4,7},{5,4},{6,5},{7,6},{8,11},{9,8},{10,9... | collective-permute-start | bytes 445448 | tf_op jit(solution)/shard_map/ppermute | solution.py:393
  94.1 4.5 %collective-permute-done.17 = bf16[40,1856]{1,0:T(8,128)(2,1)S(1)} collective-permute-done((bf16[40,1856]{1,0:T(8,128)(2,1)S(1)}, bf16[40,1856]{1,0:T(8,128)(2,1)S(1)}, u32[]{:S(2)}, u32[]{:S(2)}) %collective-permute-start.17) | collective-permute-done | bytes 148512 | tf_op jit(solution)/shard_map/ppermute | solution.py:393
  (54 shorter events, 12.0 us)
Async XLA Ops:
  21.0 8.3 %collective-permute-start = (bf16[960,512]{1,0:T(8,128)(2,1)}, bf16[960,512]{1,0:T(8,128)(2,1)S(1)}, u32[]{:S(2)}, u32[]{:S(2)}) collective-permute-start(bf16[960,512]{1,0:T(8,128)(2,1)} %get-tuple-element.45.right_ref), channel_id=1, source_target_pairs={{0,4},{4,0},{8,12},{12,8},{16,20},{20,16},{24,28},{28,24},{1,5},{5... | collective-permute-start | bytes 2949128 | tf_op jit(solution)/shard_map/ppermute | solution.py:478
  21.5 7.7 %collective-permute-start.1 = (bf16[4,160,640]{2,1,0:T(8,128)(2,1)}, bf16[4,160,640]{2,1,0:T(8,128)(2,1)S(1)}, u32[]{:S(2)}, u32[]{:S(2)}) collective-permute-start(bf16[4,160,640]{2,1,0:T(8,128)(2,1)} %get-tuple-element.46), channel_id=1, source_target_pairs={{0,4},{4,0},{8,12},{12,8},{16,20},{20,16},{24,28},{28,24},{1,5},{5... | collective-permute-start | bytes 2457608 | tf_op jit(solution)/shard_map/ppermute | solution.py:478
  21.6 7.6 %collective-permute-start.2 = (bf16[4,160,512]{2,1,0:T(8,128)(2,1)}, bf16[4,160,512]{2,1,0:T(8,128)(2,1)S(1)}, u32[]{:S(2)}, u32[]{:S(2)}) collective-permute-start(bf16[4,160,512]{2,1,0:T(8,128)(2,1)} %get-tuple-element.47), channel_id=1, source_target_pairs={{0,4},{4,0},{8,12},{12,8},{16,20},{20,16},{24,28},{28,24},{1,5},{5... | collective-permute-start | bytes 1966088 | tf_op jit(solution)/shard_map/ppermute | solution.py:478
  22.0 7.4 %copy-start.3 = (bf16[960,512]{1,0:T(8,128)(2,1)S(1)}, bf16[960,512]{1,0:T(8,128)(2,1)}, u32[]{:S(2)}) copy-start(bf16[960,512]{1,0:T(8,128)(2,1)} %get-tuple-element.45.right_ref) | copy-start | bytes 2949124
  22.0 7.4 %copy-start.4 = (bf16[4,160,640]{2,1,0:T(8,128)(2,1)S(1)}, bf16[4,160,640]{2,1,0:T(8,128)(2,1)}, u32[]{:S(2)}) copy-start(bf16[4,160,640]{2,1,0:T(8,128)(2,1)} %get-tuple-element.55.keep_ref) | copy-start | bytes 2457604
  29.2 6.0 %copy-start = (bf16[4,160,512]{2,1,0:T(8,128)(2,1)S(1)}, bf16[4,160,512]{2,1,0:T(8,128)(2,1)}, u32[]{:S(2)}) copy-start(bf16[4,160,512]{2,1,0:T(8,128)(2,1)} %get-tuple-element.61.keep_ref) | copy-start | bytes 1966084
  29.2 6.0 %copy-start.2 = (bf16[1024,512]{1,0:T(8,128)(2,1)S(1)}, bf16[1024,512]{1,0:T(8,128)(2,1)}, u32[]{:S(2)}) copy-start(bf16[1024,512]{1,0:T(8,128)(2,1)} %get-tuple-element.53.right_ref) | copy-start | bytes 3145732
  29.2 2.9 %collective-permute-start.3 = (bf16[1024,512]{1,0:T(8,128)(2,1)}, bf16[1024,512]{1,0:T(8,128)(2,1)S(1)}, u32[]{:S(2)}, u32[]{:S(2)}) collective-permute-start(bf16[1024,512]{1,0:T(8,128)(2,1)} %get-tuple-element.53.right_ref), channel_id=1, source_target_pairs={{0,4},{4,0},{8,12},{12,8},{16,20},{20,16},{24,28},{28,24},{1,5},{5... | collective-permute-start | bytes 3145736 | tf_op jit(solution)/shard_map/ppermute | solution.py:478
  32.2 6.1 %collective-permute-start.5 = (bf16[1856,512]{1,0:T(8,128)(2,1)S(1)}, bf16[1856,512]{1,0:T(8,128)(2,1)S(1)}, u32[]{:S(2)}, u32[]{:S(2)}) collective-permute-start(bf16[1856,512]{1,0:T(8,128)(2,1)S(1)} %copy-done.1), channel_id=1, source_target_pairs={{0,4},{4,0},{8,12},{12,8},{16,20},{20,16},{24,28},{28,24},{1,5},{5... | collective-permute-start | bytes 5701640 | tf_op jit(solution)/shard_map/ppermute | solution.py:478
  32.3 18.0 %collective-permute-start.4 = (bf16[2,160,1024]{2,1,0:T(8,128)(2,1)S(1)}, bf16[2,160,1024]{2,1,0:T(8,128)(2,1)}, u32[]{:S(2)}, u32[]{:S(2)}) collective-permute-start(bf16[2,160,1024]{2,1,0:T(8,128)(2,1)S(1)} %get-tuple-element.60), channel_id=1, source_target_pairs={{0,8},{4,12},{8,0},{12,4},{16,24},{20,28},{24,16},{28,20},{1,9},{5... | collective-permute-start | bytes 1966088 | tf_op jit(solution)/shard_map/ppermute | solution.py:325
  36.8 17.2 %collective-permute-start.7 = (bf16[2,160,1024]{2,1,0:T(8,128)(2,1)S(1)}, bf16[2,160,1024]{2,1,0:T(8,128)(2,1)}, u32[]{:S(2)}, u32[]{:S(2)}) collective-permute-start(bf16[2,160,1024]{2,1,0:T(8,128)(2,1)S(1)} %get-tuple-element.71), channel_id=1, source_target_pairs={{0,16},{4,20},{8,24},{12,28},{16,0},{20,4},{24,8},{28,12},{1,17},{... | collective-permute-start | bytes 1966088 | tf_op jit(solution)/shard_map/ppermute | solution.py:325
  41.2 12.7 %copy-start.5 = (bf16[2,160,896]{2,1,0:T(8,128)(2,1)}, bf16[2,160,896]{2,1,0:T(8,128)(2,1)S(1)}, u32[]{:S(2)}) copy-start(bf16[2,160,896]{2,1,0:T(8,128)(2,1)S(1)} %get-tuple-element.76) | copy-start | bytes 1720324
  52.2 10.8 %collective-permute-start.6 = (bf16[160,1024]{1,0:T(8,128)(2,1)}, bf16[160,1024]{1,0:T(8,128)(2,1)S(1)}, u32[]{:S(2)}, u32[]{:S(2)}) collective-permute-start(bf16[160,1024]{1,0:T(8,128)(2,1)} %fusion.5), channel_id=1, source_target_pairs={{0,16},{4,20},{8,24},{12,28},{16,0},{20,4},{24,8},{28,12},{1,17},{... | collective-permute-start | bytes 983048 | tf_op jit(solution)/shard_map/ppermute | solution.py:353
  55.7 11.0 %collective-permute-start.8 = (bf16[160,1024]{1,0:T(8,128)(2,1)}, bf16[160,1024]{1,0:T(8,128)(2,1)}, u32[]{:S(2)}, u32[]{:S(2)}) collective-permute-start(bf16[160,1024]{1,0:T(8,128)(2,1)} %fusion.7), channel_id=1, source_target_pairs={{0,8},{4,12},{8,0},{12,4},{16,24},{20,28},{24,16},{28,20},{1,9},{5... | collective-permute-start | bytes 983048 | tf_op jit(solution)/shard_map/ppermute | solution.py:353
  57.2 20.7 %collective-permute-start.14 = (bf16[2,160,960]{2,1,0:T(8,128)(2,1)S(1)}, bf16[2,160,960]{2,1,0:T(8,128)(2,1)S(1)}, u32[]{:S(2)}, u32[]{:S(2)}) collective-permute-start(bf16[2,160,960]{2,1,0:T(8,128)(2,1)S(1)} %get-tuple-element.78), channel_id=1, source_target_pairs={{0,16},{4,20},{8,24},{12,28},{16,0},{20,4},{24,8},{28,12},{1,17},{... | collective-permute-start | bytes 1843208 | tf_op jit(solution)/shard_map/ppermute | solution.py:325
  57.7 19.1 %collective-permute-start.12 = (bf16[2,160,896]{2,1,0:T(8,128)(2,1)}, bf16[2,160,896]{2,1,0:T(8,128)(2,1)S(1)}, u32[]{:S(2)}, u32[]{:S(2)}) collective-permute-start(bf16[2,160,896]{2,1,0:T(8,128)(2,1)} %copy-done.5), channel_id=1, source_target_pairs={{0,8},{4,12},{8,0},{12,4},{16,24},{20,28},{24,16},{28,20},{1,9},{5... | collective-permute-start | bytes 1720328 | tf_op jit(solution)/shard_map/ppermute | solution.py:325
  68.0 17.7 %collective-permute-start.11 = (bf16[40,2048]{1,0:T(8,128)(2,1)S(1)}, bf16[40,2048]{1,0:T(8,128)(2,1)S(1)}, u32[]{:S(2)}, u32[]{:S(2)}) collective-permute-start(bf16[40,2048]{1,0:T(8,128)(2,1)S(1)} %pad_maximum_fusion.3), channel_id=1, source_target_pairs={{0,3},{1,0},{2,1},{3,2},{4,7},{5,4},{6,5},{7,6},{8,11},{9,8},{10,9... | collective-permute-start | bytes 491528 | tf_op jit(solution)/shard_map/ppermute | solution.py:393
  71.7 14.0 %collective-permute-start.10 = (bf16[40,2048]{1,0:T(8,128)(2,1)S(1)}, bf16[40,2048]{1,0:T(8,128)(2,1)S(1)}, u32[]{:S(2)}, u32[]{:S(2)}) collective-permute-start(bf16[40,2048]{1,0:T(8,128)(2,1)S(1)} %pad_maximum_fusion.2), channel_id=1, source_target_pairs={{0,2},{1,3},{2,0},{3,1},{4,6},{5,7},{6,4},{7,5},{8,10},{9,11},{10,... | collective-permute-start | bytes 491528 | tf_op jit(solution)/shard_map/ppermute | solution.py:393
  76.9 6.9 %collective-permute-start.13 = (bf16[160,896]{1,0:T(8,128)(2,1)S(1)}, bf16[160,896]{1,0:T(8,128)(2,1)S(1)}, u32[]{:S(2)}, u32[]{:S(2)}) collective-permute-start(bf16[160,896]{1,0:T(8,128)(2,1)S(1)} %fusion.11), channel_id=1, source_target_pairs={{0,16},{4,20},{8,24},{12,28},{16,0},{20,4},{24,8},{28,12},{1,17},{... | collective-permute-start | bytes 860168 | tf_op jit(solution)/shard_map/ppermute | solution.py:353
  78.1 7.5 %collective-permute-start.15 = (bf16[160,960]{1,0:T(8,128)(2,1)S(1)}, bf16[160,960]{1,0:T(8,128)(2,1)S(1)}, u32[]{:S(2)}, u32[]{:S(2)}) collective-permute-start(bf16[160,960]{1,0:T(8,128)(2,1)S(1)} %fusion.9), channel_id=1, source_target_pairs={{0,8},{4,12},{8,0},{12,4},{16,24},{20,28},{24,16},{28,20},{1,9},{5... | collective-permute-start | bytes 921608 | tf_op jit(solution)/shard_map/ppermute | solution.py:353
  79.2 7.2 %collective-permute-start.9 = (bf16[40,2048]{1,0:T(8,128)(2,1)S(1)}, bf16[40,2048]{1,0:T(8,128)(2,1)S(1)}, u32[]{:S(2)}, u32[]{:S(2)}) collective-permute-start(bf16[40,2048]{1,0:T(8,128)(2,1)S(1)} %pad_maximum_fusion.1), channel_id=1, source_target_pairs={{0,1},{1,2},{2,3},{3,0},{4,5},{5,6},{6,7},{7,4},{8,9},{9,10},{10,1... | collective-permute-start | bytes 491528 | tf_op jit(solution)/shard_map/ppermute | solution.py:393
  86.5 7.6 %collective-permute-start.16 = (bf16[40,1856]{1,0:T(8,128)(2,1)S(1)}, bf16[40,1856]{1,0:T(8,128)(2,1)S(1)}, u32[]{:S(2)}, u32[]{:S(2)}) collective-permute-start(bf16[40,1856]{1,0:T(8,128)(2,1)S(1)} %pad_maximum_fusion.4), channel_id=1, source_target_pairs={{0,1},{1,2},{2,3},{3,0},{4,5},{5,6},{6,7},{7,4},{8,9},{9,10},{10,1... | collective-permute-start | bytes 445448 | tf_op jit(solution)/shard_map/ppermute | solution.py:393
  87.5 11.1 %collective-permute-start.17 = (bf16[40,1856]{1,0:T(8,128)(2,1)S(1)}, bf16[40,1856]{1,0:T(8,128)(2,1)S(1)}, u32[]{:S(2)}, u32[]{:S(2)}) collective-permute-start(bf16[40,1856]{1,0:T(8,128)(2,1)S(1)} %pad_maximum_fusion.5), channel_id=1, source_target_pairs={{0,2},{1,3},{2,0},{3,1},{4,6},{5,7},{6,4},{7,5},{8,10},{9,11},{10,... | collective-permute-start | bytes 445448 | tf_op jit(solution)/shard_map/ppermute | solution.py:393
  90.1 8.5 %collective-permute-start.18 = (bf16[40,1856]{1,0:T(8,128)(2,1)S(1)}, bf16[40,1856]{1,0:T(8,128)(2,1)S(1)}, u32[]{:S(2)}, u32[]{:S(2)}) collective-permute-start(bf16[40,1856]{1,0:T(8,128)(2,1)S(1)} %pad_maximum_fusion.6), channel_id=1, source_target_pairs={{0,3},{1,0},{2,1},{3,2},{4,7},{5,4},{6,5},{7,6},{8,11},{9,8},{10,9... | collective-permute-start | bytes 445448 | tf_op jit(solution)/shard_map/ppermute | solution.py:393
  (1 other events, 3.0 us)

commit v4 on v2

--- a/solution.py
+++ b/solution.py
@@ -8,7 +8,7 @@
 from jax.sharding import PartitionSpec as P
 
 HEADS = 12
-STAGE = 4
+SIDE_FORWARD, SIDE_BACKWARD = 12, 12
 JOIN = 4
 PAIR = 2
 LANES = 128
@@ -122,17 +122,17 @@
                 packed_ref[pair, part, at:at + size, :] = found[:, pair * block:(pair + 1) * block]
     give(2, packed_ref, packed_hbm)
 
-    @pl.loop(0, pairs)
+    @pl.loop(0, pairs, unroll=2)
     def _(pair):
         here = pl.ds(pl.multiple_of(pair * block, block), block)
         key_at = lax.broadcasted_iota(jnp.int32, (block, block), 0)
         query_at = lax.broadcasted_iota(jnp.int32, (block, block), 1)
         allowed = alive_of(key_at, live_ref[0, PAIR * pair], live_ref[0, PAIR * pair + 1], group)
         allowed = allowed & ((key_at // group) % PAIR == (query_at // group) % PAIR)
-        for first in range(0, HEADS, STAGE):
+        for first in range(0, HEADS, SIDE_FORWARD):
             spans = [
                 slice(head * head_width, (head + 1) * head_width)
-                for head in range(first, first + STAGE)
+                for head in range(first, first + SIDE_FORWARD)
             ]
             scores = [
                 dot(packed_ref[pair, 1, span, :], packed_ref[pair, 0, span, :], 0, 0)
@@ -161,15 +161,14 @@
     gain_sum_ref[...] = jnp.zeros_like(gain_sum_ref)
     load_cot.wait()
 
-    @pl.loop(0, pairs)
-    def _(pair):
+    for pair in range(pairs):
         row_at = lax.broadcasted_iota(jnp.int32, (strip, 1), 0)
         alive = alive_of(row_at, live_ref[0, PAIR * pair], live_ref[0, PAIR * pair + 1], group)
         alive = jnp.where(alive, 1.0, 0.0)
         gain = gain_ref[...].reshape(1, model_width)
-        out_rows = pl.ds(pl.multiple_of(pair * strip, strip), strip)
+        out_rows = slice(pair * strip, (pair + 1) * strip)
         for turn in range(JOIN):
-            here = pl.ds(pl.multiple_of(pair * block + turn * strip, strip), strip)
+            here = slice(pair * block + turn * strip, pair * block + (turn + 1) * strip)
             columns = slice(turn * model_width, (turn + 1) * model_width)
             attended = rows_ref[here, :]
             power = jnp.mean(attended * attended, axis=1, keepdims=True)
@@ -220,8 +219,8 @@
                 at += taken
             at -= ref.shape[0]
 
-    for first in range(0, heads, STAGE):
-        together = range(first, first + STAGE)
+    for first in range(0, heads, SIDE_BACKWARD):
+        together = range(first, first + SIDE_BACKWARD)
         spans = [slice(head * head_width, (head + 1) * head_width) for head in together]
         probs = [probs_ref[0, head] for head in together]
         d_probs = [

time: 99.8 us -> 97.1 us (0.973)
  Pallas kernels: 33.6 us -> 30.9 us
    pallas_call x1, Pallas kernels: 19.4 us -> 17.6 us  [run_forward(): pl.pallas_call(forward_kernel, out_shape=[jax.ShapeDtypeStruct(s, BF16) f...]
where the time goes in v4:
time: 97.1 us; the launch traced here: 96.7 us
  waiting for transfers between devices  33 us (34%)
  Pallas kernels  30.9 us (32%)
  starting transfers between devices  23 us (24%)
  other arithmetic  7.48 us (8%)
  local copies, waits for them, and re-layouts  1.53 us (2%)
    pallas_call x1, Pallas kernels, run_forward(): pl.pallas_call(forward_kernel, out_shape=[jax.ShapeDtypeStruct(s, BF16) f...  17.6 us
    ppermute x4, waiting for transfers between devices, first(): lax.ppermute(sent, 'dp', flip_pairs(self.ranks, self.order[0]))  14.2 us
    ppermute x4, waiting for transfers between devices, step(): self.got = [lax.ppermute(sent, 'dp', flip_pairs(self.ranks, axis))]  11.4 us
    ppermute x6, starting transfers between devices, __init__(): self.got.append(lax.ppermute(row_of(k), 'vis', pairs))  10.4 us
    pallas_call x1, Pallas kernels, run_backward(): pl.pallas_call(backward_kernel, out_shape=[jax.ShapeDtypeStruct((h, pairs...  7.18 us
    ppermute x6, waiting for transfers between devices, __init__(): self.got.append(lax.ppermute(row_of(k), 'vis', pairs))  6.27 us
    pallas_call x3, Pallas kernels, product(): pl.pallas_call(functools.partial(product_kernel, pieces=taken, extra_at=e...  6.1 us
    ppermute x4, starting transfers between devices, first(): lax.ppermute(sent, 'dp', flip_pairs(self.ranks, self.order[0]))  5.96 us
  transfers between devices with their start and end apart: 19, of which 10 were waited for; matrix products, arithmetic and copies ran while one was open for 8% of the time, Pallas kernels for 14%

profile of v4, /device:TPU:0, one launch (start us, length us, event | category | flops | bytes accessed | tf_op | source)
XLA Modules:
  0.0 96.7 jit_solution(4614247301213568566)
XLA Ops:
  0.6 17.6 %shard_map.102 = (bf16[128,5120]{1,0:T(8,128)(2,1)}, bf16[4,3,960,128]{3,2,1,0:T(8,128)(2,1)}, bf16[4,12,128,128]{3,2,1,0:T(8,128)(2,1)}, bf16[4,960,128]{2,1,0:...) custom-call(s32[1]{0:T(128)} %bitcast.rank_ref, ...), custom_call_target="tpu_custom_call" | custom-call | flops 1 | bytes 1 | tf_op jit(solution)/shard_map/pallas_call | solution.py:417
  19.3 7.2 %shard_map.103 = (bf16[1024,512]{1,0:T(8,128)(2,1)}, bf16[1856,512]{1,0:T(8,128)(2,1)}) custom-call(bf16[4,3,960,128]{3,2,1,0:T(8,128)(2,1)} %get-tuple-element.48.packed_ref, bf16[4,12,128,128]{3,2,1,0:T(8,128)(2,1)} %get-tuple-element.49.probs_ref, bf16[4,960,128]{2,1,0:T(8,128)(2,1)} %get-tuple-element.50.d_context_ref), custom_call_target="tpu_custom_call" | custom-call | flops 1 | bytes 1 | tf_op jit(solution)/shard_map/pallas_call | solution.py:443
  26.6 1.6 %shard_map.104 = (bf16[2,160,1024]{2,1,0:T(8,128)(2,1)S(1)}, bf16[2,160,1024]{2,1,0:T(8,128)(2,1)S(1)}) custom-call(bf16[4,160,640]{2,1,0:T(8,128)(2,1)S(1)} %copy-done.4, bf16[4,160,640]{2,1,0:T(8,128)(2,1)S(1)} %collective-permute-done.1.other_ref, bf16[960,512]{1,0:T(8,128)(2,1)S(1)} %copy-done.3, bf16[960,512]{1,0:T(8,128)(2,1)S(1)} %collective-permute-done.right_other_ref), custom_call_target="tpu_custom_call" | custom-call | flops 1 | bytes 1 | tf_op jit(solution)/shard_map/pallas_call | solution.py:287
  28.3 1.1 %collective-permute-done.3.right_other_ref = bf16[1024,512]{1,0:T(8,128)(2,1)S(1)} collective-permute-done((bf16[1024,512]{1,0:T(8,128)(2,1)}, bf16[1024,512]{1,0:T(8,128)(2,1)S(1)}, u32[]{:S(2)}, u32[]{:S(2)}) %collective-permute-start.3) | collective-permute-done | bytes 1048608 | tf_op jit(solution)/shard_map/ppermute | solution.py:472
  29.5 2.9 %collective-permute-start.4 = (bf16[2,160,1024]{2,1,0:T(8,128)(2,1)S(1)}, bf16[2,160,1024]{2,1,0:T(8,128)(2,1)}, u32[]{:S(2)}, u32[]{:S(2)}) collective-permute-start(bf16[2,160,1024]{2,1,0:T(8,128)(2,1)S(1)} %get-tuple-element.60), channel_id=1, source_target_pairs={{0,8},{4,12},{8,0},{12,4},{16,24},{20,28},{24,16},{28,20},{1,9},{5... | collective-permute-start | bytes 1966088 | tf_op jit(solution)/shard_map/ppermute | solution.py:319
  32.4 1.5 %shard_map.105 = (bf16[2,160,1024]{2,1,0:T(8,128)(2,1)S(1)}, bf16[2,160,1024]{2,1,0:T(8,128)(2,1)S(1)}) custom-call(bf16[4,160,512]{2,1,0:T(8,128)(2,1)S(1)} %copy-done, bf16[4,160,512]{2,1,0:T(8,128)(2,1)S(1)} %collective-permute-done.2.other_ref, bf16[1024,512]{1,0:T(8,128)(2,1)S(1)} %copy-done.2, bf16[1024,512]{1,0:T(8,128)(2,1)S(1)} %collective-permute-done.3.right_other_ref), custom_call_target="tpu_custom_call" | custom-call | flops 1 | bytes 1 | tf_op jit(solution)/shard_map/pallas_call | solution.py:287
  34.0 1.6 %collective-permute-start.7 = (bf16[2,160,1024]{2,1,0:T(8,128)(2,1)S(1)}, bf16[2,160,1024]{2,1,0:T(8,128)(2,1)}, u32[]{:S(2)}, u32[]{:S(2)}) collective-permute-start(bf16[2,160,1024]{2,1,0:T(8,128)(2,1)S(1)} %get-tuple-element.71), channel_id=1, source_target_pairs={{0,16},{4,20},{8,24},{12,28},{16,0},{20,4},{24,8},{28,12},{1,17},{... | collective-permute-start | bytes 1966088 | tf_op jit(solution)/shard_map/ppermute | solution.py:319
  35.5 2.9 %shard_map.106 = (bf16[2,160,896]{2,1,0:T(8,128)(2,1)S(1)}, bf16[2,160,896]{2,1,0:T(8,128)(2,1)S(1)}, bf16[2,160,960]{2,1,0:T(8,128)(2,1)S(1)}, bf16[2,160,960]{2,1,0:T(8,128)(2,1)S(1)}) custom-call(bf16[4,160,512]{2,1,0:T(8,128)(2,1)S(1)} %copy-done, bf16[4,160,512]{2,1,0:T(8,128)(2,1)S(1)} %collective-permute-done.2.other_ref, ...), custom_call_target="tpu_custom_call" | custom-call | flops 1 | bytes 1 | tf_op jit(solution)/shard_map/pallas_call | solution.py:287
  38.5 9.1 %collective-permute-done.4 = bf16[2,160,1024]{2,1,0:T(8,128)(2,1)} collective-permute-done((bf16[2,160,1024]{2,1,0:T(8,128)(2,1)S(1)}, bf16[2,160,1024]{2,1,0:T(8,128)(2,1)}, u32[]{:S(2)}, u32[]{:S(2)}) %collective-permute-start.4) | collective-permute-done | bytes 655392 | tf_op jit(solution)/shard_map/ppermute | solution.py:319
  47.5 1.8 %fusion.5 = bf16[160,1024]{1,0:T(8,128)(2,1)} fusion(bf16[2,160,1024]{2,1,0:T(8,128)(2,1)} %collective-permute-done.4, bf16[2,160,1024]{2,1,0:T(8,128)(2,1)S(1)} %get-tuple-element.59), kind=kLoop, calls=%fused_computation.18 | loop fusion | flops 655360 | bytes 983040 | tf_op jit(solution)/shard_map/convert_element_type | solution.py:354
  49.4 1.8 %collective-permute-start.6 = (bf16[160,1024]{1,0:T(8,128)(2,1)}, bf16[160,1024]{1,0:T(8,128)(2,1)S(1)}, u32[]{:S(2)}, u32[]{:S(2)}) collective-permute-start(bf16[160,1024]{1,0:T(8,128)(2,1)} %fusion.5), channel_id=1, source_target_pairs={{0,16},{4,20},{8,24},{12,28},{16,0},{20,4},{24,8},{28,12},{1,17},{... | collective-permute-start | bytes 983048 | tf_op jit(solution)/shard_map/ppermute | solution.py:347
  51.2 1.8 %fusion.7 = bf16[160,1024]{1,0:T(8,128)(2,1)} fusion(bf16[2,160,1024]{2,1,0:T(8,128)(2,1)} %collective-permute-done.7, bf16[2,160,1024]{2,1,0:T(8,128)(2,1)S(1)} %get-tuple-element.70), kind=kLoop, calls=%fused_computation.20 | loop fusion | flops 655360 | bytes 983040 | tf_op jit(solution)/shard_map/convert_element_type | solution.py:354
  53.0 1.5 %collective-permute-start.8 = (bf16[160,1024]{1,0:T(8,128)(2,1)}, bf16[160,1024]{1,0:T(8,128)(2,1)}, u32[]{:S(2)}, u32[]{:S(2)}) collective-permute-start(bf16[160,1024]{1,0:T(8,128)(2,1)} %fusion.7), channel_id=1, source_target_pairs={{0,8},{4,12},{8,0},{12,4},{16,24},{20,28},{24,16},{28,20},{1,9},{5... | collective-permute-start | bytes 983048 | tf_op jit(solution)/shard_map/ppermute | solution.py:347
  56.0 4.2 %collective-permute-done.6 = bf16[160,1024]{1,0:T(8,128)(2,1)S(1)} collective-permute-done((bf16[160,1024]{1,0:T(8,128)(2,1)}, bf16[160,1024]{1,0:T(8,128)(2,1)S(1)}, u32[]{:S(2)}, u32[]{:S(2)}) %collective-permute-start.6) | collective-permute-done | bytes 327712 | tf_op jit(solution)/shard_map/ppermute | solution.py:347
  61.4 2.6 %collective-permute-done.8 = bf16[160,1024]{1,0:T(8,128)(2,1)} collective-permute-done((bf16[160,1024]{1,0:T(8,128)(2,1)}, bf16[160,1024]{1,0:T(8,128)(2,1)}, u32[]{:S(2)}, u32[]{:S(2)}) %collective-permute-start.8) | collective-permute-done | bytes 327712 | tf_op jit(solution)/shard_map/ppermute | solution.py:347
  63.9 1.2 %fusion.1 = bf16[160,1024]{1,0:T(8,128)(2,1)S(1)} fusion(bf16[160,1024]{1,0:T(8,128)(2,1)} %collective-permute-done.8, bf16[2,160,1024]{2,1,0:T(8,128)(2,1)} %collective-permute-done.7, bf16[2,160,1024]{2,1,0:T(8,128)(2,1)S(1)} %get-tuple-element.70), kind=kLoop, calls=%fused_computation.3 | loop fusion | flops 1310720 | bytes 1310720 | tf_op jit(solution)/shard_map/convert_element_type | solution.py:364
  65.2 3.6 %collective-permute-start.11 = (bf16[40,2048]{1,0:T(8,128)(2,1)S(1)}, bf16[40,2048]{1,0:T(8,128)(2,1)S(1)}, u32[]{:S(2)}, u32[]{:S(2)}) collective-permute-start(bf16[40,2048]{1,0:T(8,128)(2,1)S(1)} %pad_maximum_fusion.3), channel_id=1, source_target_pairs={{0,3},{1,0},{2,1},{3,2},{4,7},{5,4},{6,5},{7,6},{8,11},{9,8},{10,9... | collective-permute-start | bytes 491528 | tf_op jit(solution)/shard_map/ppermute | solution.py:387
  69.0 5.1 %collective-permute-done.12 = bf16[2,160,896]{2,1,0:T(8,128)(2,1)S(1)} collective-permute-done((bf16[2,160,896]{2,1,0:T(8,128)(2,1)}, bf16[2,160,896]{2,1,0:T(8,128)(2,1)S(1)}, u32[]{:S(2)}, u32[]{:S(2)}) %collective-permute-start.12) | collective-permute-done | bytes 573472 | tf_op jit(solution)/shard_map/ppermute | solution.py:319
  76.4 1.6 %collective-permute-start.9 = (bf16[40,2048]{1,0:T(8,128)(2,1)S(1)}, bf16[40,2048]{1,0:T(8,128)(2,1)S(1)}, u32[]{:S(2)}, u32[]{:S(2)}) collective-permute-start(bf16[40,2048]{1,0:T(8,128)(2,1)S(1)} %pad_maximum_fusion.1), channel_id=1, source_target_pairs={{0,1},{1,2},{2,3},{3,0},{4,5},{5,6},{6,7},{7,4},{8,9},{9,10},{10,1... | collective-permute-start | bytes 491528 | tf_op jit(solution)/shard_map/ppermute | solution.py:387
  78.1 3.0 %collective-permute-done.13 = bf16[160,896]{1,0:T(8,128)(2,1)S(1)} collective-permute-done((bf16[160,896]{1,0:T(8,128)(2,1)S(1)}, bf16[160,896]{1,0:T(8,128)(2,1)S(1)}, u32[]{:S(2)}, u32[]{:S(2)}) %collective-permute-start.13) | collective-permute-done | bytes 286752 | tf_op jit(solution)/shard_map/ppermute | solution.py:347
  81.2 1.5 %collective-permute-done.15 = bf16[160,960]{1,0:T(8,128)(2,1)S(1)} collective-permute-done((bf16[160,960]{1,0:T(8,128)(2,1)S(1)}, bf16[160,960]{1,0:T(8,128)(2,1)S(1)}, u32[]{:S(2)}, u32[]{:S(2)}) %collective-permute-start.15) | collective-permute-done | bytes 307232 | tf_op jit(solution)/shard_map/ppermute | solution.py:347
  84.7 2.6 %collective-permute-start.17 = (bf16[40,1856]{1,0:T(8,128)(2,1)S(1)}, bf16[40,1856]{1,0:T(8,128)(2,1)S(1)}, u32[]{:S(2)}, u32[]{:S(2)}) collective-permute-start(bf16[40,1856]{1,0:T(8,128)(2,1)S(1)} %pad_maximum_fusion.5), channel_id=1, source_target_pairs={{0,2},{1,3},{2,0},{3,1},{4,6},{5,7},{6,4},{7,5},{8,10},{9,11},{10,... | collective-permute-start | bytes 445448 | tf_op jit(solution)/shard_map/ppermute | solution.py:387
  87.4 1.4 %collective-permute-start.18 = (bf16[40,1856]{1,0:T(8,128)(2,1)S(1)}, bf16[40,1856]{1,0:T(8,128)(2,1)S(1)}, u32[]{:S(2)}, u32[]{:S(2)}) collective-permute-start(bf16[40,1856]{1,0:T(8,128)(2,1)S(1)} %pad_maximum_fusion.6), channel_id=1, source_target_pairs={{0,3},{1,0},{2,1},{3,2},{4,7},{5,4},{6,5},{7,6},{8,11},{9,8},{10,9... | collective-permute-start | bytes 445448 | tf_op jit(solution)/shard_map/ppermute | solution.py:387
  91.3 4.5 %collective-permute-done.17 = bf16[40,1856]{1,0:T(8,128)(2,1)S(1)} collective-permute-done((bf16[40,1856]{1,0:T(8,128)(2,1)S(1)}, bf16[40,1856]{1,0:T(8,128)(2,1)S(1)}, u32[]{:S(2)}, u32[]{:S(2)}) %collective-permute-start.17) | collective-permute-done | bytes 148512 | tf_op jit(solution)/shard_map/ppermute | solution.py:387
  (54 shorter events, 11.9 us)
Async XLA Ops:
  18.2 8.2 %collective-permute-start = (bf16[960,512]{1,0:T(8,128)(2,1)}, bf16[960,512]{1,0:T(8,128)(2,1)S(1)}, u32[]{:S(2)}, u32[]{:S(2)}) collective-permute-start(bf16[960,512]{1,0:T(8,128)(2,1)} %get-tuple-element.45.right_ref), channel_id=1, source_target_pairs={{0,4},{4,0},{8,12},{12,8},{16,20},{20,16},{24,28},{28,24},{1,5},{5... | collective-permute-start | bytes 2949128 | tf_op jit(solution)/shard_map/ppermute | solution.py:472
  18.7 7.7 %collective-permute-start.1 = (bf16[4,160,640]{2,1,0:T(8,128)(2,1)}, bf16[4,160,640]{2,1,0:T(8,128)(2,1)S(1)}, u32[]{:S(2)}, u32[]{:S(2)}) collective-permute-start(bf16[4,160,640]{2,1,0:T(8,128)(2,1)} %get-tuple-element.46), channel_id=1, source_target_pairs={{0,4},{4,0},{8,12},{12,8},{16,20},{20,16},{24,28},{28,24},{1,5},{5... | collective-permute-start | bytes 2457608 | tf_op jit(solution)/shard_map/ppermute | solution.py:472
  18.8 7.6 %collective-permute-start.2 = (bf16[4,160,512]{2,1,0:T(8,128)(2,1)}, bf16[4,160,512]{2,1,0:T(8,128)(2,1)S(1)}, u32[]{:S(2)}, u32[]{:S(2)}) collective-permute-start(bf16[4,160,512]{2,1,0:T(8,128)(2,1)} %get-tuple-element.47), channel_id=1, source_target_pairs={{0,4},{4,0},{8,12},{12,8},{16,20},{20,16},{24,28},{28,24},{1,5},{5... | collective-permute-start | bytes 1966088 | tf_op jit(solution)/shard_map/ppermute | solution.py:472
  19.2 7.4 %copy-start.3 = (bf16[960,512]{1,0:T(8,128)(2,1)S(1)}, bf16[960,512]{1,0:T(8,128)(2,1)}, u32[]{:S(2)}) copy-start(bf16[960,512]{1,0:T(8,128)(2,1)} %get-tuple-element.45.right_ref) | copy-start | bytes 2949124
  19.3 7.4 %copy-start.4 = (bf16[4,160,640]{2,1,0:T(8,128)(2,1)S(1)}, bf16[4,160,640]{2,1,0:T(8,128)(2,1)}, u32[]{:S(2)}) copy-start(bf16[4,160,640]{2,1,0:T(8,128)(2,1)} %get-tuple-element.55.keep_ref) | copy-start | bytes 2457604
  26.4 6.0 %copy-start = (bf16[4,160,512]{2,1,0:T(8,128)(2,1)S(1)}, bf16[4,160,512]{2,1,0:T(8,128)(2,1)}, u32[]{:S(2)}) copy-start(bf16[4,160,512]{2,1,0:T(8,128)(2,1)} %get-tuple-element.61.keep_ref) | copy-start | bytes 1966084
  26.4 6.0 %copy-start.2 = (bf16[1024,512]{1,0:T(8,128)(2,1)S(1)}, bf16[1024,512]{1,0:T(8,128)(2,1)}, u32[]{:S(2)}) copy-start(bf16[1024,512]{1,0:T(8,128)(2,1)} %get-tuple-element.53.right_ref) | copy-start | bytes 3145732
  26.5 2.9 %collective-permute-start.3 = (bf16[1024,512]{1,0:T(8,128)(2,1)}, bf16[1024,512]{1,0:T(8,128)(2,1)S(1)}, u32[]{:S(2)}, u32[]{:S(2)}) collective-permute-start(bf16[1024,512]{1,0:T(8,128)(2,1)} %get-tuple-element.53.right_ref), channel_id=1, source_target_pairs={{0,4},{4,0},{8,12},{12,8},{16,20},{20,16},{24,28},{28,24},{1,5},{5... | collective-permute-start | bytes 3145736 | tf_op jit(solution)/shard_map/ppermute | solution.py:472
  29.4 6.1 %collective-permute-start.5 = (bf16[1856,512]{1,0:T(8,128)(2,1)S(1)}, bf16[1856,512]{1,0:T(8,128)(2,1)S(1)}, u32[]{:S(2)}, u32[]{:S(2)}) collective-permute-start(bf16[1856,512]{1,0:T(8,128)(2,1)S(1)} %copy-done.1), channel_id=1, source_target_pairs={{0,4},{4,0},{8,12},{12,8},{16,20},{20,16},{24,28},{28,24},{1,5},{5... | collective-permute-start | bytes 5701640 | tf_op jit(solution)/shard_map/ppermute | solution.py:472
  29.5 18.0 %collective-permute-start.4 = (bf16[2,160,1024]{2,1,0:T(8,128)(2,1)S(1)}, bf16[2,160,1024]{2,1,0:T(8,128)(2,1)}, u32[]{:S(2)}, u32[]{:S(2)}) collective-permute-start(bf16[2,160,1024]{2,1,0:T(8,128)(2,1)S(1)} %get-tuple-element.60), channel_id=1, source_target_pairs={{0,8},{4,12},{8,0},{12,4},{16,24},{20,28},{24,16},{28,20},{1,9},{5... | collective-permute-start | bytes 1966088 | tf_op jit(solution)/shard_map/ppermute | solution.py:319
  34.0 17.2 %collective-permute-start.7 = (bf16[2,160,1024]{2,1,0:T(8,128)(2,1)S(1)}, bf16[2,160,1024]{2,1,0:T(8,128)(2,1)}, u32[]{:S(2)}, u32[]{:S(2)}) collective-permute-start(bf16[2,160,1024]{2,1,0:T(8,128)(2,1)S(1)} %get-tuple-element.71), channel_id=1, source_target_pairs={{0,16},{4,20},{8,24},{12,28},{16,0},{20,4},{24,8},{28,12},{1,17},{... | collective-permute-start | bytes 1966088 | tf_op jit(solution)/shard_map/ppermute | solution.py:319
  38.5 12.7 %copy-start.5 = (bf16[2,160,896]{2,1,0:T(8,128)(2,1)}, bf16[2,160,896]{2,1,0:T(8,128)(2,1)S(1)}, u32[]{:S(2)}) copy-start(bf16[2,160,896]{2,1,0:T(8,128)(2,1)S(1)} %get-tuple-element.76) | copy-start | bytes 1720324
  49.4 10.8 %collective-permute-start.6 = (bf16[160,1024]{1,0:T(8,128)(2,1)}, bf16[160,1024]{1,0:T(8,128)(2,1)S(1)}, u32[]{:S(2)}, u32[]{:S(2)}) collective-permute-start(bf16[160,1024]{1,0:T(8,128)(2,1)} %fusion.5), channel_id=1, source_target_pairs={{0,16},{4,20},{8,24},{12,28},{16,0},{20,4},{24,8},{28,12},{1,17},{... | collective-permute-start | bytes 983048 | tf_op jit(solution)/shard_map/ppermute | solution.py:347
  53.0 11.0 %collective-permute-start.8 = (bf16[160,1024]{1,0:T(8,128)(2,1)}, bf16[160,1024]{1,0:T(8,128)(2,1)}, u32[]{:S(2)}, u32[]{:S(2)}) collective-permute-start(bf16[160,1024]{1,0:T(8,128)(2,1)} %fusion.7), channel_id=1, source_target_pairs={{0,8},{4,12},{8,0},{12,4},{16,24},{20,28},{24,16},{28,20},{1,9},{5... | collective-permute-start | bytes 983048 | tf_op jit(solution)/shard_map/ppermute | solution.py:347
  54.4 20.7 %collective-permute-start.14 = (bf16[2,160,960]{2,1,0:T(8,128)(2,1)S(1)}, bf16[2,160,960]{2,1,0:T(8,128)(2,1)S(1)}, u32[]{:S(2)}, u32[]{:S(2)}) collective-permute-start(bf16[2,160,960]{2,1,0:T(8,128)(2,1)S(1)} %get-tuple-element.78), channel_id=1, source_target_pairs={{0,16},{4,20},{8,24},{12,28},{16,0},{20,4},{24,8},{28,12},{1,17},{... | collective-permute-start | bytes 1843208 | tf_op jit(solution)/shard_map/ppermute | solution.py:319
  55.0 19.1 %collective-permute-start.12 = (bf16[2,160,896]{2,1,0:T(8,128)(2,1)}, bf16[2,160,896]{2,1,0:T(8,128)(2,1)S(1)}, u32[]{:S(2)}, u32[]{:S(2)}) collective-permute-start(bf16[2,160,896]{2,1,0:T(8,128)(2,1)} %copy-done.5), channel_id=1, source_target_pairs={{0,8},{4,12},{8,0},{12,4},{16,24},{20,28},{24,16},{28,20},{1,9},{5... | collective-permute-start | bytes 1720328 | tf_op jit(solution)/shard_map/ppermute | solution.py:319
  65.2 17.7 %collective-permute-start.11 = (bf16[40,2048]{1,0:T(8,128)(2,1)S(1)}, bf16[40,2048]{1,0:T(8,128)(2,1)S(1)}, u32[]{:S(2)}, u32[]{:S(2)}) collective-permute-start(bf16[40,2048]{1,0:T(8,128)(2,1)S(1)} %pad_maximum_fusion.3), channel_id=1, source_target_pairs={{0,3},{1,0},{2,1},{3,2},{4,7},{5,4},{6,5},{7,6},{8,11},{9,8},{10,9... | collective-permute-start | bytes 491528 | tf_op jit(solution)/shard_map/ppermute | solution.py:387
  68.9 14.0 %collective-permute-start.10 = (bf16[40,2048]{1,0:T(8,128)(2,1)S(1)}, bf16[40,2048]{1,0:T(8,128)(2,1)S(1)}, u32[]{:S(2)}, u32[]{:S(2)}) collective-permute-start(bf16[40,2048]{1,0:T(8,128)(2,1)S(1)} %pad_maximum_fusion.2), channel_id=1, source_target_pairs={{0,2},{1,3},{2,0},{3,1},{4,6},{5,7},{6,4},{7,5},{8,10},{9,11},{10,... | collective-permute-start | bytes 491528 | tf_op jit(solution)/shard_map/ppermute | solution.py:387
  74.2 6.9 %collective-permute-start.13 = (bf16[160,896]{1,0:T(8,128)(2,1)S(1)}, bf16[160,896]{1,0:T(8,128)(2,1)S(1)}, u32[]{:S(2)}, u32[]{:S(2)}) collective-permute-start(bf16[160,896]{1,0:T(8,128)(2,1)S(1)} %fusion.11), channel_id=1, source_target_pairs={{0,16},{4,20},{8,24},{12,28},{16,0},{20,4},{24,8},{28,12},{1,17},{... | collective-permute-start | bytes 860168 | tf_op jit(solution)/shard_map/ppermute | solution.py:347
  75.3 7.5 %collective-permute-start.15 = (bf16[160,960]{1,0:T(8,128)(2,1)S(1)}, bf16[160,960]{1,0:T(8,128)(2,1)S(1)}, u32[]{:S(2)}, u32[]{:S(2)}) collective-permute-start(bf16[160,960]{1,0:T(8,128)(2,1)S(1)} %fusion.9), channel_id=1, source_target_pairs={{0,8},{4,12},{8,0},{12,4},{16,24},{20,28},{24,16},{28,20},{1,9},{5... | collective-permute-start | bytes 921608 | tf_op jit(solution)/shard_map/ppermute | solution.py:347
  76.4 7.2 %collective-permute-start.9 = (bf16[40,2048]{1,0:T(8,128)(2,1)S(1)}, bf16[40,2048]{1,0:T(8,128)(2,1)S(1)}, u32[]{:S(2)}, u32[]{:S(2)}) collective-permute-start(bf16[40,2048]{1,0:T(8,128)(2,1)S(1)} %pad_maximum_fusion.1), channel_id=1, source_target_pairs={{0,1},{1,2},{2,3},{3,0},{4,5},{5,6},{6,7},{7,4},{8,9},{9,10},{10,1... | collective-permute-start | bytes 491528 | tf_op jit(solution)/shard_map/ppermute | solution.py:387
  83.7 7.6 %collective-permute-start.16 = (bf16[40,1856]{1,0:T(8,128)(2,1)S(1)}, bf16[40,1856]{1,0:T(8,128)(2,1)S(1)}, u32[]{:S(2)}, u32[]{:S(2)}) collective-permute-start(bf16[40,1856]{1,0:T(8,128)(2,1)S(1)} %pad_maximum_fusion.4), channel_id=1, source_target_pairs={{0,1},{1,2},{2,3},{3,0},{4,5},{5,6},{6,7},{7,4},{8,9},{9,10},{10,1... | collective-permute-start | bytes 445448 | tf_op jit(solution)/shard_map/ppermute | solution.py:387
  84.7 11.1 %collective-permute-start.17 = (bf16[40,1856]{1,0:T(8,128)(2,1)S(1)}, bf16[40,1856]{1,0:T(8,128)(2,1)S(1)}, u32[]{:S(2)}, u32[]{:S(2)}) collective-permute-start(bf16[40,1856]{1,0:T(8,128)(2,1)S(1)} %pad_maximum_fusion.5), channel_id=1, source_target_pairs={{0,2},{1,3},{2,0},{3,1},{4,6},{5,7},{6,4},{7,5},{8,10},{9,11},{10,... | collective-permute-start | bytes 445448 | tf_op jit(solution)/shard_map/ppermute | solution.py:387
  87.4 8.5 %collective-permute-start.18 = (bf16[40,1856]{1,0:T(8,128)(2,1)S(1)}, bf16[40,1856]{1,0:T(8,128)(2,1)S(1)}, u32[]{:S(2)}, u32[]{:S(2)}) collective-permute-start(bf16[40,1856]{1,0:T(8,128)(2,1)S(1)} %pad_maximum_fusion.6), channel_id=1, source_target_pairs={{0,3},{1,0},{2,1},{3,2},{4,7},{5,4},{6,5},{7,6},{8,11},{9,8},{10,9... | collective-permute-start | bytes 445448 | tf_op jit(solution)/shard_map/ppermute | solution.py:387
  (1 other events, 3.0 us)
